TPU v7x, 768 devices: a whole 4x8x12 slice. The times are simulated.
768 devices in a mesh: dom: 64 (over x, y, core), grp: 12 (over z).
Axes of the slice: x: 4, y: 8, z: 12, core: 2. Of those that a mesh axis runs over, the one named last changes fastest.
Arguments:
- features: bfloat16 [1572864, 256], P(('dom', 'grp')), may hold values from -6 to 6
- weight: bfloat16 [256, 256], replicated, may hold values from -0.375 to 0.375
- cotangent: bfloat16 [1572864, 256], P(('dom', 'grp')), may hold values from -6 to 6
- edge_index: int32 [1572864, 8], P(('dom', 'grp')), may hold values from 0 to 5631
- edge_weight: float32 [1572864, 8], P(('dom', 'grp')), may hold values from 0.1 to 0.6
- send_rows: int32 [49152, 32], P(('dom', 'grp')), may hold values from 0 to 2047
- counts: int32 [49152], P(('dom', 'grp')), may hold values from 1 to 32
- boundary: int32 [98304], P(('dom', 'grp')), may hold values from 0 to 2047
- skip_flags: int32 [64, 12], P('dom'), may hold values 0 or 1
- cached_panels: bfloat16 [64, 12, 128, 256], P('dom'), may hold values from -6 to 6
Outputs:
- activated: bfloat16 [1572864, 256], P(('dom', 'grp'))
- feature_grad: bfloat16 [1572864, 256], P(('dom', 'grp'))
- weight_grad: float32 [256, 256], replicated
Inputs may be any that keep to these rules, and one draw needn't show every extreme that they name: `edge_index`: rows below 2048 are the device's own nodes, the next 2048 are arrived in order of sender, the rest the panels in order of owner; slots past a block's count are zero rows. `send_rows`: indices of the sender's own rows; repeats allowed. `boundary`: indices of the owner's own rows; repeats allowed.
All inputs are finite; a program needn't handle non-finite values. No bound on the sum of `skip_flags` on one device may be relied on, other than what follows from the above.
Results may differ from a plain program's by a relative error of at most 0.014.
Values may be sent and summed in bfloat16 or wider, within the bound.
No kernel may reach another device: no remote copies, remote signals or barrier semaphores. Data moves between devices by JAX's collectives and lax.ppermute only.
A program may use at most 64 MiB of HBM per device.

v0:
```python
import math

import jax
import jax.numpy as jnp
from jax import lax
from jax.sharding import PartitionSpec as P


def activation(values):
    return jax.nn.gelu(values, approximate=True)


def aggregate(source_table, edge_index, edge_weight, block_rows):
    node_count, fanout = edge_index.shape
    blocks = node_count // block_rows

    def one_block(inputs):
        index_block, weight_block = inputs
        picked = source_table[index_block]
        return jnp.sum(weight_block[:, :, None] * picked.astype(jnp.float32), axis=1)

    summed = lax.map(
        one_block,
        (
            edge_index.reshape(blocks, block_rows, fanout),
            edge_weight.reshape(blocks, block_rows, fanout),
        ),
    )
    return summed.reshape(node_count, source_table.shape[1])


def spread_back(grad_pre, edge_index, edge_weight, table_rows, block_rows):
    node_count = edge_index.shape[0]
    hidden_width = grad_pre.shape[1]

    def add_block(number, running):
        offset = number * block_rows
        index_block = lax.dynamic_slice_in_dim(edge_index, offset, block_rows, 0)
        weight_block = lax.dynamic_slice_in_dim(edge_weight, offset, block_rows, 0)
        grad_block = lax.dynamic_slice_in_dim(grad_pre, offset, block_rows, 0).astype(jnp.float32)
        contrib = weight_block[:, :, None] * grad_block[:, None, :]
        return running.at[index_block.reshape(-1)].add(contrib.reshape(-1, hidden_width))

    return lax.fori_loop(
        0, node_count // block_rows, add_block, jnp.zeros((table_rows, hidden_width), jnp.float32)
    )


def shards(
    features,
    weight,
    cotangent,
    edge_index,
    edge_weight,
    send_rows,
    counts,
    boundary,
    skip_flags,
    cached_panels,
):
    node_count, hidden_width = features.shape
    peer_count = lax.axis_size("dom")
    group_count = lax.axis_size("grp")
    slot_count = send_rows.shape[1]
    panel_count = boundary.shape[0]
    block_rows = min(512, node_count)
    remote_rows = peer_count * slot_count
    remote_end = node_count + remote_rows
    table_rows = remote_end + group_count * panel_count
    live_slots = lax.broadcasted_iota(jnp.int32, send_rows.shape, 1) < counts[:, None]
    skipped = (skip_flags[0] == 1)[:, None, None]
    blank = jnp.zeros((), jnp.bfloat16)
    projected = jnp.dot(features, weight, preferred_element_type=jnp.float32).astype(jnp.bfloat16)
    outgoing = jnp.where(live_slots[:, :, None], projected[send_rows], blank)
    arrived = lax.all_to_all(outgoing, "dom", split_axis=0, concat_axis=0, tiled=True)
    arrived = arrived.reshape(remote_rows, hidden_width)
    fresh = lax.all_gather(projected[boundary][None], "grp", axis=0, tiled=True)
    stale = cached_panels[0]
    source_table = jnp.concatenate(
        [projected, arrived, jnp.where(skipped, stale, fresh).reshape(-1, hidden_width)], axis=0
    )
    preact = aggregate(source_table, edge_index, edge_weight, block_rows)
    activated = activation(preact).astype(jnp.bfloat16)
    _, pullback = jax.vjp(activation, preact)
    grad_pre = pullback(cotangent.astype(jnp.float32))[0].astype(jnp.bfloat16)
    table_grad = spread_back(grad_pre, edge_index, edge_weight, table_rows, block_rows)
    remote_grad = (
        table_grad[node_count:remote_end]
        .reshape(peer_count, slot_count, hidden_width)
        .astype(jnp.bfloat16)
    )
    returned = lax.all_to_all(remote_grad, "dom", split_axis=0, concat_axis=0, tiled=True)
    panel_grad = jnp.where(
        skipped, 0.0, table_grad[remote_end:].reshape(group_count, panel_count, hidden_width)
    ).astype(jnp.bfloat16)
    owner_grad = lax.psum_scatter(panel_grad, "grp", scatter_dimension=0, tiled=True).astype(
        jnp.float32
    )
    back_terms = jnp.where(live_slots[:, :, None], returned.astype(jnp.float32), 0.0)
    local_grad = (
        table_grad[:node_count]
        .at[send_rows.reshape(-1)]
        .add(back_terms.reshape(remote_rows, hidden_width))
    )
    local_grad = local_grad.at[boundary].add(owner_grad[0])
    grad_proj = local_grad.astype(jnp.bfloat16)
    feature_grad = jnp.dot(grad_proj, weight.T, preferred_element_type=jnp.float32).astype(
        jnp.bfloat16
    )
    weight_term = lax.dot_general(
        features, grad_proj, (((0,), (0,)), ((), ())), preferred_element_type=jnp.float32
    )
    total_nodes = node_count * peer_count * group_count
    weight_grad = lax.psum(weight_term, ("dom", "grp")) * (1.0 / math.sqrt(total_nodes))
    return (activated, feature_grad, weight_grad)


def solution(mesh):
    in_specs = (
        P(("dom", "grp"), None),
        P(),
        P(("dom", "grp"), None),
        P(("dom", "grp"), None),
        P(("dom", "grp"), None),
        P(("dom", "grp"), None),
        P(("dom", "grp")),
        P(("dom", "grp")),
        P("dom", None),
        P("dom", None, None, None),
    )
    out_specs = (P(("dom", "grp"), None), P(("dom", "grp"), None), P())
    return jax.shard_map(shards, mesh=mesh, in_specs=in_specs, out_specs=out_specs, check_vma=False)
```

profile of v0, /device:TPU:1, one launch (start us, length us, event | category | flops | bytes accessed | tf_op | source)
XLA Modules:
  0.0 840.9 jit_solution(15890538439688338115)
XLA Ops:
  10.2 7.5 gather_fusion.1
  19.0 14.7 %all-to-all-start = ((bf16[64,32,256]{2,1,0:T(8,128)(2,1)}), bf16[64,32,256]{2,1,0:T(8,128)(2,1)S(1)}, u32[]{:S(2)}, u32[]{:S(2)}) async-start(bf16[64,32,256]{2,1,0:T(8,128)(2,1)} %broadcast_select_fusion), calls=%async_computation | async-start | bytes 2097152 | tf_op jit(solution)/shard_map/all_to_all | solution.py:75
  37.3 29.5 %all-gather = bf16[1536,256]{1,0:T(8,128)(2,1)S(1)} all-gather(bf16[128,256]{1,0:T(8,128)(2,1)S(1)} %gather_fusion.2), channel_id=2, replica_groups=mesh['dom'=64,'grp'=12] {'grp'}, dimensions={0}, use_global_device_ids=true | all-gather | bytes 851968 | tf_op jit(solution)/shard_map/all_gather | solution.py:77
  69.0 2.9 pad_maximum_fusion
  71.9 84.0 %while.23 = (s32[]{:T(128)}, f32[4,512,256]{2,1,0:T(8,128)}, f32[4,512,8]{2,1,0:T(8,128)}, s32[4,512,8]{2,1,0:T(8,128)}, bf16[5632,256]{1,0:T(8,128)(2,1)}, /*index=5*/s32[]{:T(128)}) while((s32[]{:T(128)}, f32[4,512,256]{2,1,0:T(8,128)}, f32[4,512,8]{2,1,0:T(8,128)}, s32[4,512,8]{2,1,0:T(8,128)}, bf16[5632,256]{1,0:T(8,128)(2,1)}, ...), condition=%wide.region_2.3_spmd, body=%wide.region_0.2_spmd.sunk | while | flops 3031042 | bytes 8028249 | solution.py:22
  73.0 15.2 %gather_fusion = bf16[4096,256]{1,0:T(8,128)(2,1)S(1)} fusion(bf16[5632,256]{1,0:T(8,128)(2,1)} %get-tuple-element.237, s32[4096]{0:T(1024)S(1)} %broadcast_clamp_fusion.3), kind=kCustom, calls=%fused_computation.clone.1 | custom fusion | bytes 4210688 | tf_op jit(solution)/shard_map/while/body/eval_jaxpr/gather | solution.py:19
  89.2 2.8 fusion.25
  94.0 15.2 %gather_fusion = bf16[4096,256]{1,0:T(8,128)(2,1)S(1)} fusion(bf16[5632,256]{1,0:T(8,128)(2,1)} %get-tuple-element.237, s32[4096]{0:T(1024)S(1)} %broadcast_clamp_fusion.3), kind=kCustom, calls=%fused_computation.clone.1 | custom fusion | bytes 4210688 | tf_op jit(solution)/shard_map/while/body/eval_jaxpr/gather | solution.py:19
  110.2 2.8 fusion.25
  115.0 15.2 %gather_fusion = bf16[4096,256]{1,0:T(8,128)(2,1)S(1)} fusion(bf16[5632,256]{1,0:T(8,128)(2,1)} %get-tuple-element.237, s32[4096]{0:T(1024)S(1)} %broadcast_clamp_fusion.3), kind=kCustom, calls=%fused_computation.clone.1 | custom fusion | bytes 4210688 | tf_op jit(solution)/shard_map/while/body/eval_jaxpr/gather | solution.py:19
  136.0 15.2 %gather_fusion = bf16[4096,256]{1,0:T(8,128)(2,1)S(1)} fusion(bf16[5632,256]{1,0:T(8,128)(2,1)} %get-tuple-element.237, s32[4096]{0:T(1024)S(1)} %broadcast_clamp_fusion.3), kind=kCustom, calls=%fused_computation.clone.1 | custom fusion | bytes 4210688 | tf_op jit(solution)/shard_map/while/body/eval_jaxpr/gather | solution.py:19
  155.9 4.5 fusion.6
  160.4 2.9 broadcast_in_dim.83
  163.2 127.5 %while.24 = (s32[]{:T(128)}, f32[5632,256]{1,0:T(8,128)}, s32[2048,8]{1,0:T(8,128)}, f32[2048,8]{1,0:T(8,128)}, bf16[2048,256]{1,0:T(8,128)(2,1)S(1)}, /*index=5*/s32[]{:T(128)}, s32[]{:T(128)}, s32[]{:T(128)}, s32[]{:T(128)}) while((s32[]{:T(128)}, f32[5632,256]{1,0:T(8,128)}, s32[2048,8]{1,0:T(8,128)}, f32[2048,8]{1,0:T(8,128)}, ...), condition=%wide.region_5.6_spmd, body=%wide.region_3.5_spmd.sunk | while | flops 2240518 | bytes 7258271 | solution.py:44
  165.6 29.5 %scatter_custom_fusion.8 = f32[5632,256]{1,0:T(8,128)} fusion(f32[5632,256]{1,0:T(8,128)} %get-tuple-element.249, s32[4096]{0:T(1024)S(1)} %bitcast.74, f32[512,256]{1,0:T(8,128)S(1)} %dynamic-slice_convert_fusion.2, f32[4096]{0:T(1024)S(1)} %mul.208), kind=kCustom, calls=%fused_computation.13.clone.1 | custom fusion | flops 2097152 | bytes 6307840 | tf_op jit(solution)/shard_map/while/body/eval_jaxpr/scatter-add | solution.py:42
  197.5 29.5 %scatter_custom_fusion.8 = f32[5632,256]{1,0:T(8,128)} fusion(f32[5632,256]{1,0:T(8,128)} %get-tuple-element.249, s32[4096]{0:T(1024)S(1)} %bitcast.74, f32[512,256]{1,0:T(8,128)S(1)} %dynamic-slice_convert_fusion.2, f32[4096]{0:T(1024)S(1)} %mul.208), kind=kCustom, calls=%fused_computation.13.clone.1 | custom fusion | flops 2097152 | bytes 6307840 | tf_op jit(solution)/shard_map/while/body/eval_jaxpr/scatter-add | solution.py:42
  229.3 29.5 %scatter_custom_fusion.8 = f32[5632,256]{1,0:T(8,128)} fusion(f32[5632,256]{1,0:T(8,128)} %get-tuple-element.249, s32[4096]{0:T(1024)S(1)} %bitcast.74, f32[512,256]{1,0:T(8,128)S(1)} %dynamic-slice_convert_fusion.2, f32[4096]{0:T(1024)S(1)} %mul.208), kind=kCustom, calls=%fused_computation.13.clone.1 | custom fusion | flops 2097152 | bytes 6307840 | tf_op jit(solution)/shard_map/while/body/eval_jaxpr/scatter-add | solution.py:42
  261.2 29.5 %scatter_custom_fusion.8 = f32[5632,256]{1,0:T(8,128)} fusion(f32[5632,256]{1,0:T(8,128)} %get-tuple-element.249, s32[4096]{0:T(1024)S(1)} %bitcast.74, f32[512,256]{1,0:T(8,128)S(1)} %dynamic-slice_convert_fusion.2, f32[4096]{0:T(1024)S(1)} %mul.208), kind=kCustom, calls=%fused_computation.13.clone.1 | custom fusion | flops 2097152 | bytes 6307840 | tf_op jit(solution)/shard_map/while/body/eval_jaxpr/scatter-add | solution.py:42
  293.4 15.4 %all-to-all-start.1 = ((bf16[64,32,256]{2,1,0:T(8,128)(2,1)}), bf16[64,32,256]{2,1,0:T(8,128)(2,1)}, u32[]{:S(2)}, u32[]{:S(2)}) async-start(bf16[64,32,256]{2,1,0:T(8,128)(2,1)} %bitcast.16), calls=%async_computation.1 | async-start | bytes 2097152 | tf_op jit(solution)/shard_map/all_to_all | solution.py:92
  313.7 23.6 %all-to-all-done.1 = bf16[64,32,256]{2,1,0:T(8,128)(2,1)} async-done(((bf16[64,32,256]{2,1,0:T(8,128)(2,1)}), bf16[64,32,256]{2,1,0:T(8,128)(2,1)}, u32[]{:S(2)}, u32[]{:S(2)}) %all-to-all-start.1) | async-done | bytes 1048608 | tf_op jit(solution)/shard_map/all_to_all | solution.py:92
  337.3 2.9 convert_select_fusion
  340.2 12.7 %scatter_fusion = f32[2048,256]{1,0:T(8,128)S(1)} fusion(f32[2048,256]{1,0:T(8,128)S(1)} %slice.10, s32[2048]{0:T(1024)S(1)} %bitcast.75, f32[2048,256]{1,0:T(8,128)} %bitcast.68), kind=kCustom, calls=%fused_computation.4 | custom fusion | flops 524288 | bytes 6299648 | tf_op jit(solution)/shard_map/scatter-add | solution.py:103
  352.9 4.5 reduce-scatter.2.cloned.1.call-done
  362.4 469.8 %all-reduce.2.cloned.1.call-done = f32[256,256]{0,1:T(8,128)} async-done(((f32[256,256]{0,1:T(8,128)}), f32[256,256]{0,1:T(8,128)}) %all-reduce.2.cloned.1.call-update) | async-done | bytes 262160 | tf_op jit(solution)/shard_map/psum | solution.py:114
  (92 shorter events, 51.1 us)
Async XLA Ops:
  7.2 1.7 copy-start
  17.8 16.0 %copy-start.2 = (f32[2048,8]{0,1:T(8,128)S(1)}, f32[2048,8]{0,1:T(8,128)}, u32[]{:S(2)}) copy-start(f32[2048,8]{0,1:T(8,128)} %param.18) | copy-start | bytes 196612
  19.0 16.1 %copy-start.3 = (s32[2048,8]{0,1:T(8,128)S(1)}, s32[2048,8]{0,1:T(8,128)}, u32[]{:S(2)}) copy-start(s32[2048,8]{0,1:T(8,128)} %param.17) | copy-start | bytes 196612
  19.0 17.4 %copy-start.5 = (s32[128]{0:T(128)S(1)}, s32[128]{0:T(128)}, u32[]{:S(2)}) copy-start(s32[128]{0:T(128)} %param.21) | copy-start | bytes 1540
  19.0 18.3 %copy-start.6 = (s32[1,12]{1,0:T(1,128)S(1)}, s32[1,12]{1,0:T(1,128)}, u32[]{:S(2)}) copy-start(s32[1,12]{1,0:T(1,128)} %param.22) | copy-start | bytes 148
  19.0 50.0 %all-to-all-start = ((bf16[64,32,256]{2,1,0:T(8,128)(2,1)}), bf16[64,32,256]{2,1,0:T(8,128)(2,1)S(1)}, u32[]{:S(2)}, u32[]{:S(2)}) async-start(bf16[64,32,256]{2,1,0:T(8,128)(2,1)} %broadcast_select_fusion), calls=%async_computation | async-start | bytes 2097152 | tf_op jit(solution)/shard_map/all_to_all | solution.py:75
  293.4 43.8 %all-to-all-start.1 = ((bf16[64,32,256]{2,1,0:T(8,128)(2,1)}), bf16[64,32,256]{2,1,0:T(8,128)(2,1)}, u32[]{:S(2)}, u32[]{:S(2)}) async-start(bf16[64,32,256]{2,1,0:T(8,128)(2,1)} %bitcast.16), calls=%async_computation.1 | async-start | bytes 2097152 | tf_op jit(solution)/shard_map/all_to_all | solution.py:92
  308.8 3.0 copy-start.4
  308.8 48.6 %reduce-scatter.2.cloned.1.call-start = ((), (), s32[]{:S(2)}) async-start(), calls=%async_computation.3 | async-start | bytes 851968 | tf_op jit(solution)/shard_map/reduce_scatter | solution.py:96
  311.7 520.5 %all-reduce.2.cloned.1.call-start = ((), (), s32[]{:S(2)}) async-start(), calls=%async_computation.4 | async-start | bytes 524288 | tf_op jit(solution)/shard_map/psum | solution.py:114
  359.8 1.2 copy-start.1
Sparse Core Ops, SparseCore 0:
  312.7 44.6 reduce-scatter.1
  364.3 467.8 all-reduce.1
where the time goes:
time: 842 us; the launch traced here: 841 us
  waiting for transfers between devices  498 us (59%)
  other arithmetic  166 us (20%)
  local copies, waits for them, and re-layouts  98.5 us (12%)
  starting transfers between devices  30.4 us (4%)
  blocking collectives  29.5 us (4%)
  between operations  14.2 us (2%)
    psum x1, waiting for transfers between devices, shards(): lax.psum(weight_term, ('dom', 'grp')) * (1.0 / math.sqrt(total_nodes))  470 us
    scatter-add x4, other arithmetic, add_block(): running.at[index_block.reshape(-1)].add(contrib.reshape(-1, hidden_width))  118 us
    gather x4, local copies, waits for them, and re-layouts, one_block(): picked = source_table[index_block]  60.7 us
    all_gather x1, blocking collectives, shards(): fresh = lax.all_gather(projected[boundary][None], 'grp', axis=0, tiled=True)  29.5 us
    all_to_all x1, waiting for transfers between devices, shards(): lax.all_to_all(remote_grad, 'dom', split_axis=0, concat_axis=0, tiled=True)  23.6 us
  transfers between devices with their start and end apart: 4, of which 3 were waited for; matrix products, arithmetic and copies ran while one was open for 3% of the time, Pallas kernels for 0%

commit v1 on v0

v1 whole, which is shorter than its diff:
```python
import functools
import math

import jax
import jax.numpy as jnp
from jax import lax
from jax.experimental import pallas as pl
from jax.experimental.pallas import tpu as pltpu
from jax.sharding import PartitionSpec as P

BF16 = jnp.bfloat16
F32 = jnp.float32
BLOCK = 256
LANES = 128
MIB = 1 << 20
GELU_SCALE = math.sqrt(2.0 / math.pi)
GELU_CUBE = 0.044715


def contract(left, right, left_dim, right_dim):
    return lax.dot_general(
        left, right, (((left_dim,), (right_dim,)), ((), ())), preferred_element_type=F32
    )


def call(kernel, outs, *operands, **options):
    return pl.pallas_call(kernel, out_shape=outs, **options)(*operands)


def shape(dims, dtype):
    return jax.ShapeDtypeStruct(dims, dtype)


VMEM = pl.BlockSpec(memory_space=pltpu.VMEM)
SMEM = pl.BlockSpec(memory_space=pltpu.SMEM)
ANY = pl.BlockSpec(memory_space=pl.ANY)


def small_iota(dims, dim):
    return lax.broadcasted_iota(jnp.int32, dims, dim).astype(jnp.int16)


def one_hot(index, count):
    rows = index.shape[0]
    splat = jnp.broadcast_to(index, (rows, LANES)).astype(jnp.int16)
    lane = small_iota((rows, LANES), 1)
    tiles = []
    for tile in range(count // LANES):
        hit = splat == lane + jnp.int16(tile * LANES)
        tiles.append(jnp.where(hit, jnp.ones((), BF16), jnp.zeros((), BF16)))
    return jnp.concatenate(tiles, axis=1)


def gather_kernel(send_ref, counts_ref, bound_ref, feat_ref, out_ref, panel_ref):
    slots, peers = send_ref.shape
    nodes = feat_ref.shape[0]
    live = lax.broadcasted_iota(jnp.int32, (slots, peers), 0) < counts_ref[...]
    send = jnp.where(live, send_ref[...], -1)
    panel = bound_ref.shape[1]
    bound = jnp.transpose(jnp.broadcast_to(bound_ref[...], (panel, panel)))[:, :1]
    panel_ref[...] = jnp.dot(
        one_hot(bound, nodes), feat_ref[...], preferred_element_type=F32
    ).astype(BF16)
    group = BLOCK // slots
    for part in range(peers // group):
        index = jnp.concatenate(
            [send[:, peer : peer + 1] for peer in range(part * group, (part + 1) * group)], axis=0
        )
        out_ref[part * BLOCK : (part + 1) * BLOCK, :] = jnp.dot(
            one_hot(index, nodes), feat_ref[...], preferred_element_type=F32
        ).astype(BF16)


def build_kernel(
    own_blocks,
    index_ref,
    edge_weight_ref,
    feat_ref,
    weight_ref,
    cot_ref,
    cached_ref,
    mixer_ref,
    local_ref,
    cot_out_ref,
    cached_out_ref,
    index_rep,
    weight_rep,
    projected,
):
    step = pl.program_id(0)
    slots, nodes = index_ref.shape

    @pl.when(step == 0)
    def _():
        index = index_ref[...]
        merged = []
        for slot in range(slots):
            same = index == index[slot : slot + 1]
            merged.append(
                jnp.sum(jnp.where(same, edge_weight_ref[...], 0.0), axis=0, keepdims=True)
            )
        for slot in range(slots):
            index_rep[slot] = jnp.broadcast_to(index[slot : slot + 1], (16, nodes)).astype(
                jnp.int16
            )
            weight_rep[slot] = jnp.broadcast_to(merged[slot], (16, nodes)).astype(BF16)
        projected[...] = contract(weight_ref[...], feat_ref[...], 0, 1).astype(BF16)
        cot_out_ref[...] = jnp.transpose(cot_ref[...])
        cached_out_ref[...] = jnp.transpose(cached_ref[...])
        local_ref[...] = jnp.zeros_like(local_ref)

    def tile(number, carry):
        lanes = pl.ds(pl.multiple_of(number * LANES, LANES), LANES)
        index = [index_rep[slot, :, lanes] for slot in range(slots)]
        weights = [weight_rep[slot, :, lanes] for slot in range(slots)]
        row = (lax.broadcasted_iota(jnp.int32, (16, LANES), 0) + step * BLOCK).astype(jnp.int16)
        for sub in range(BLOCK // 16):
            here = row + jnp.int16(sub * 16)
            value = jnp.zeros((16, LANES), BF16)
            for slot in range(slots):
                value = jnp.where(index[slot] == here, weights[slot], value)
            mixer_ref[sub * 16 : sub * 16 + 16, lanes] = value
        return carry

    lax.fori_loop(0, nodes // LANES, tile, 0)

    @pl.when(step < own_blocks)
    def _():
        columns = pl.ds(pl.multiple_of(step * BLOCK, BLOCK), BLOCK)
        local_ref[...] += jnp.dot(
            projected[:, columns], mixer_ref[...], preferred_element_type=F32
        )


def middle_kernel(
    first_row,
    skip_ref,
    arrived_ref,
    fresh_ref,
    cached_ref,
    weight_ref,
    local_ref,
    cot_ref,
    mixer_ref,
    act_ref,
    grad_ref,
    remote_ref,
    panel_ref,
    mixer,
    table,
    sems,
):
    rows, nodes = mixer.shape
    groups = skip_ref.shape[0]
    remote = arrived_ref.shape[0]
    panel = fresh_ref.shape[0] // groups
    blocks = nodes // BLOCK

    def load(number):
        lanes = pl.ds(pl.multiple_of(number * BLOCK, BLOCK), BLOCK)
        return pltpu.make_async_copy(
            mixer_ref.at[pl.ds(first_row, rows), lanes], mixer.at[:, lanes], sems.at[number]
        )

    for number in range(blocks):
        load(number).start()
    for start in range(0, remote, 512):
        table[:, start : start + 512] = contract(
            weight_ref[...], arrived_ref[start : start + 512, :], 0, 1
        ).astype(BF16)
    for group in range(groups):
        fresh = contract(
            weight_ref[...], fresh_ref[group * panel : (group + 1) * panel, :], 0, 1
        ).astype(BF16)
        stale = cached_ref[:, group * panel : (group + 1) * panel]
        table[:, remote + group * panel : remote + (group + 1) * panel] = jnp.where(
            skip_ref[group] == 1, stale, fresh
        )

    def forward(number, carry):
        load(number).wait()
        lanes = pl.ds(pl.multiple_of(number * BLOCK, BLOCK), BLOCK)
        x = local_ref[:, lanes] + jnp.dot(
            table[...], mixer[:, lanes], preferred_element_type=F32
        )
        square = x * x
        bend = jnp.tanh(GELU_SCALE * x * (1.0 + GELU_CUBE * square))
        half = 0.5 * (1.0 + bend)
        act_ref[:, lanes] = (x * half).astype(BF16)
        slope = half + (0.5 * GELU_SCALE) * x * (1.0 - bend * bend) * (
            1.0 + (3.0 * GELU_CUBE) * square
        )
        grad_ref[:, lanes] = (cot_ref[:, lanes].astype(F32) * slope).astype(BF16)
        return carry

    lax.fori_loop(0, blocks, forward, 0)

    def backward(number, carry):
        start = pl.multiple_of(number * BLOCK, BLOCK)
        remote_ref[pl.ds(start, BLOCK), :] = contract(
            mixer[pl.ds(start, BLOCK), :], grad_ref[...], 1, 1
        ).astype(BF16)
        return carry

    lax.fori_loop(0, remote // BLOCK, backward, 0)
    for group in range(groups):
        start = remote + group * panel
        value = contract(mixer[start : start + panel, :], grad_ref[...], 1, 1)
        panel_ref[group * panel : (group + 1) * panel, :] = jnp.where(
            skip_ref[group] == 1, 0.0, value
        ).astype(BF16)


def local_kernel(
    mixer_ref,
    grad_ref,
    act_ref,
    feat_ref,
    arrived_ref,
    fresh_ref,
    remote_ref,
    panel_ref,
    grad_out_ref,
    term_ref,
    act_out_ref,
):
    step = pl.program_id(0)
    rows = pl.ds(pl.multiple_of(step * BLOCK, BLOCK), BLOCK)
    value = contract(mixer_ref[...], grad_ref[...], 1, 1)
    grad_out_ref[...] = value

    @pl.when(step == 0)
    def _():
        term_ref[...] = contract(arrived_ref[...], remote_ref[...], 0, 0) + contract(
            fresh_ref[...], panel_ref[...], 0, 0
        )

    term_ref[...] += contract(feat_ref[...], value.astype(BF16), 0, 0)
    act_out_ref[...] = jnp.transpose(act_ref[:, rows])


def final_kernel(
    send_ref, bound_ref, local_ref, returned_ref, owner_ref, weight_ref, out_ref, owner_pair
):
    step = pl.program_id(0)
    slots = send_ref.shape[1]
    panel = bound_ref.shape[1]

    @pl.when(step == 0)
    def _():
        total = jnp.sum(owner_ref[...].astype(F32), axis=0)
        high = total.astype(BF16)
        owner_pair[:panel] = high
        owner_pair[panel:] = (total - high.astype(F32)).astype(BF16)

    row = (lax.broadcasted_iota(jnp.int32, (BLOCK, LANES), 0) + step * BLOCK).astype(jnp.int16)

    def columns(ref, start):
        index = jnp.broadcast_to(ref[:, start : start + LANES], (BLOCK, LANES)).astype(jnp.int16)
        return jnp.where(index == row, jnp.ones((), BF16), jnp.zeros((), BF16))

    pick = jnp.concatenate(
        [columns(send_ref, start) for start in range(0, slots, LANES)], axis=1
    )
    pick_owner = jnp.concatenate(
        [columns(bound_ref, start) for start in range(0, panel, LANES)] * 2, axis=1
    )
    total = (
        local_ref[...]
        + jnp.dot(pick, returned_ref[...], preferred_element_type=F32)
        + jnp.dot(pick_owner, owner_pair[...], preferred_element_type=F32)
    )
    out_ref[...] = contract(total.astype(BF16), weight_ref[...], 1, 1).astype(BF16)


def shards(
    features,
    weight,
    cotangent,
    edge_index,
    edge_weight,
    send_rows,
    counts,
    boundary,
    skip_flags,
    cached_panels,
):
    nodes, width = features.shape
    peers = lax.axis_size("dom")
    groups = lax.axis_size("grp")
    fanout = edge_index.shape[1]
    slots = send_rows.shape[1]
    panel = boundary.shape[0]
    remote = peers * slots
    table = nodes + remote + groups * panel
    bound_row = boundary.reshape(1, panel)

    with jax.named_scope("gather_sent_rows"):
        outgoing, own_panel = call(
            gather_kernel,
            (shape((remote, width), BF16), shape((panel, width), BF16)),
            send_rows.T,
            counts.reshape(1, peers),
            bound_row,
            features,
            in_specs=[VMEM] * 4,
            out_specs=[VMEM] * 2,
            compiler_params=pltpu.CompilerParams(vmem_limit_bytes=24 * MIB),
        )
    arrived = lax.all_to_all(
        outgoing.reshape(peers, slots, width), "dom", split_axis=0, concat_axis=0, tiled=True
    ).reshape(remote, width)
    fresh = lax.all_gather(own_panel, "grp", axis=0, tiled=True)

    with jax.named_scope("build_mixer"):
        whole = lambda dims: pl.BlockSpec(dims, lambda step: (0,) * len(dims))
        mixer, local_pre, cot_t, cached_t = call(
            functools.partial(build_kernel, nodes // BLOCK),
            (
                shape((table, nodes), BF16),
                shape((width, nodes), F32),
                shape((width, nodes), BF16),
                shape((width, groups * panel), BF16),
            ),
            edge_index.T,
            edge_weight.T,
            features,
            weight,
            cotangent,
            cached_panels.reshape(groups * panel, width),
            grid=(table // BLOCK,),
            in_specs=[
                whole((fanout, nodes)),
                whole((fanout, nodes)),
                whole((nodes, width)),
                whole((width, width)),
                whole((nodes, width)),
                whole((groups * panel, width)),
            ],
            out_specs=[
                pl.BlockSpec((BLOCK, nodes), lambda step: (step, 0)),
                whole((width, nodes)),
                whole((width, nodes)),
                whole((width, groups * panel)),
            ],
            scratch_shapes=[
                pltpu.VMEM((fanout, 16, nodes), jnp.int16),
                pltpu.VMEM((fanout, 16, nodes), BF16),
                pltpu.VMEM((width, nodes), BF16),
            ],
            compiler_params=pltpu.CompilerParams(vmem_limit_bytes=30 * MIB),
            cost_estimate=pl.CostEstimate(
                flops=2 * nodes * nodes * width,
                bytes_accessed=2 * table * nodes,
                transcendentals=0,
            ),
        )

    others = table - nodes
    with jax.named_scope("forward_and_remote_grads"):
        act_t, grad_t, remote_grad, panel_grad = call(
            functools.partial(middle_kernel, nodes),
            (
                shape((width, nodes), BF16),
                shape((width, nodes), BF16),
                shape((remote, width), BF16),
                shape((groups * panel, width), BF16),
            ),
            skip_flags.reshape(groups),
            arrived,
            fresh,
            cached_t,
            weight,
            local_pre,
            cot_t,
            mixer,
            in_specs=[SMEM] + [VMEM] * 6 + [ANY],
            out_specs=[VMEM] * 4,
            scratch_shapes=[
                pltpu.VMEM((others, nodes), BF16),
                pltpu.VMEM((width, others), BF16),
                pltpu.SemaphoreType.DMA((nodes // BLOCK,)),
            ],
            compiler_params=pltpu.CompilerParams(vmem_limit_bytes=50 * MIB),
        )
    returned = lax.all_to_all(
        remote_grad.reshape(peers, slots, width), "dom", split_axis=0, concat_axis=0, tiled=True
    ).reshape(remote, width)
    owner_grad = lax.psum_scatter(
        panel_grad.reshape(groups, panel, width), "grp", scatter_dimension=0, tiled=True
    )

    with jax.named_scope("own_grads"):
        local_grad, term, activated = call(
            local_kernel,
            (shape((nodes, width), F32), shape((width, width), F32), shape((nodes, width), BF16)),
            mixer,
            grad_t,
            act_t,
            features,
            arrived,
            fresh,
            remote_grad,
            panel_grad,
            grid=(nodes // BLOCK,),
            in_specs=[
                pl.BlockSpec((BLOCK, nodes), lambda step: (step, 0)),
                whole((width, nodes)),
                whole((width, nodes)),
                pl.BlockSpec((BLOCK, width), lambda step: (step, 0)),
                whole((remote, width)),
                whole((groups * panel, width)),
                whole((remote, width)),
                whole((groups * panel, width)),
            ],
            out_specs=[
                pl.BlockSpec((BLOCK, width), lambda step: (step, 0)),
                whole((width, width)),
                pl.BlockSpec((BLOCK, width), lambda step: (step, 0)),
            ],
            compiler_params=pltpu.CompilerParams(vmem_limit_bytes=30 * MIB),
            cost_estimate=pl.CostEstimate(
                flops=2 * nodes * nodes * width + 2 * table * width * width,
                bytes_accessed=2 * nodes * nodes,
                transcendentals=0,
            ),
        )

    parts = lax.all_to_all(
        term.reshape(peers, width // peers, width), "dom", split_axis=0, concat_axis=0, tiled=True
    )
    part = jnp.sum(parts, axis=0)
    parts = lax.all_to_all(
        jnp.broadcast_to(part[None], (groups,) + part.shape),
        "grp",
        split_axis=0,
        concat_axis=0,
        tiled=True,
    )
    part = jnp.sum(parts, axis=0) * (1.0 / math.sqrt(nodes * peers * groups))
    weight_grad = lax.all_to_all(
        jnp.broadcast_to(part[None], (peers,) + part.shape),
        "dom",
        split_axis=0,
        concat_axis=0,
        tiled=True,
    ).reshape(width, width)

    live = lax.broadcasted_iota(jnp.int32, send_rows.shape, 1) < counts[:, None]
    send_row = jnp.where(live, send_rows, -1).reshape(1, remote)
    with jax.named_scope("add_returned_rows"):
        feature_grad = call(
            final_kernel,
            shape((nodes, width), BF16),
            send_row,
            bound_row,
            local_grad,
            returned,
            owner_grad,
            weight,
            grid=(nodes // BLOCK,),
            in_specs=[
                whole((1, remote)),
                whole((1, panel)),
                pl.BlockSpec((BLOCK, width), lambda step: (step, 0)),
                whole((remote, width)),
                whole(owner_grad.shape),
                whole((width, width)),
            ],
            out_specs=pl.BlockSpec((BLOCK, width), lambda step: (step, 0)),
            scratch_shapes=[pltpu.VMEM((2 * panel, width), BF16)],
            compiler_params=pltpu.CompilerParams(vmem_limit_bytes=24 * MIB),
        )
    return (activated, feature_grad, weight_grad)


def solution(mesh):
    in_specs = (
        P(("dom", "grp"), None),
        P(),
        P(("dom", "grp"), None),
        P(("dom", "grp"), None),
        P(("dom", "grp"), None),
        P(("dom", "grp"), None),
        P(("dom", "grp")),
        P(("dom", "grp")),
        P("dom", None),
        P("dom", None, None, None),
    )
    out_specs = (P(("dom", "grp"), None), P(("dom", "grp"), None), P())
    return jax.shard_map(shards, mesh=mesh, in_specs=in_specs, out_specs=out_specs, check_vma=False)
```

time: 842 us -> 268 us (0.32)
  the two profiles are of different devices: /device:TPU:1 before, /device:TPU:2 now
where the time goes in v1:
time: 268 us; the launch traced here: 267 us
  blocking collectives  87.3 us (33%)
  Pallas kernels  75.4 us (28%)
  waiting for transfers between devices  53.4 us (20%)
  starting transfers between devices  20.3 us (8%)
  local copies, waits for them, and re-layouts  16.6 us (6%)
  between operations  14.2 us (5%)
    pallas_call x5, Pallas kernels, call(): return pl.pallas_call(kernel, out_shape=outs, **options)(*operands)  75.4 us
    reduce_scatter x1, waiting for transfers between devices, shards(): lax.psum_scatter(panel_grad.reshape(groups, panel, width), 'grp', scatter...  52.7 us
    all_gather x1, blocking collectives, shards(): fresh = lax.all_gather(own_panel, 'grp', axis=0, tiled=True)  34 us
    all_to_all x1, blocking collectives, shards(): lax.all_to_all(term.reshape(peers, width // peers, width), 'dom', split_a...  21.6 us
    all_to_all x1, blocking collectives, shards(): lax.all_to_all(jnp.broadcast_to(part[None], (peers,) + part.shape), 'dom'...  18.1 us
    unnamed x48, local copies, waits for them, and re-layouts  14.6 us
    all_to_all x1, starting transfers between devices, shards(): lax.all_to_all(outgoing.reshape(peers, slots, width), 'dom', split_axis=0...  13.7 us
    all_to_all x1, blocking collectives, shards(): lax.all_to_all(jnp.broadcast_to(part[None], (groups,) + part.shape), 'grp...  13.6 us
  transfers between devices with their start and end apart: 3, of which 1 were waited for; matrix products, arithmetic and copies ran while one was open for 1% of the time, Pallas kernels for 13%

profile of v1, /device:TPU:2, one launch (start us, length us, event | category | flops | bytes accessed | tf_op | source)
XLA Modules:
  0.0 267.4 jit_solution(2347006269409885611)
XLA Ops:
  7.2 1.2 copy-done.2
  10.4 3.6 %gather_sent_rows.1 = (bf16[2048,256]{1,0:T(8,128)(2,1)}, bf16[128,256]{1,0:T(8,128)(2,1)S(1)}) custom-call(s32[32,64]{1,0:T(8,128)S(1)} %bitcast.15, s32[1,64]{1,0:T(1,128)S(1)} %bitcast.16, s32[1,128]{1,0:T(1,128)S(1)} %bitcast.17, bf16[2048,256]{1,0:T(8,128)(2,1)S(1)} %copy-done.2), custom_call_target="tpu_custom_call" | custom-call | tf_op jit(solution)/shard_map/gather_sent_rows/pallas_call | solution.py:27
  14.0 13.7 %all-to-all-start = ((bf16[64,32,256]{2,1,0:T(8,128)(2,1)}), bf16[64,32,256]{2,1,0:T(8,128)(2,1)S(1)}, u32[]{:S(2)}, u32[]{:S(2)}) async-start(bf16[64,32,256]{2,1,0:T(8,128)(2,1)} %bitcast.7), calls=%async_computation | async-start | bytes 2097152 | tf_op jit(solution)/shard_map/all_to_all | solution.py:310
  27.8 1.2 copy-done.20
  29.1 35.8 %build_mixer.1 = (bf16[5632,2048]{1,0:T(8,128)(2,1)}, f32[256,2048]{1,0:T(8,128)S(1)}, bf16[256,2048]{1,0:T(8,128)(2,1)S(1)}, bf16[256,1536]{1,0:T(8,128)(2,1)S(1)}) custom-call(s32[8,2048]{1,0:T(8,128)S(1)} %bitcast.21, f32[8,2048]{1,0:T(8,128)S(1)} %bitcast.22, bf16[2048,256]{1,0:T(8,128)(2,1)S(1)} %copy-done.3, bf16[256,256]{1,0:T(8,128)(2,1)S(1)} %copy-done.11, ...), custom_call_target="tpu_custom_call" | custom-call | flops 2147483648 | bytes 23068672 | tf_op jit(solution)/shard_map/build_mixer/pallas_call | solution.py:27
  64.9 1.4 copy-done.6
  66.3 1.0 copy-done.7
  67.3 1.0 copy-done.9
  68.2 34.0 %all_gather.3.fresh_ref = bf16[1536,256]{1,0:T(8,128)(2,1)S(1)} all-gather(bf16[128,256]{1,0:T(8,128)(2,1)S(1)} %get-tuple-element.18), channel_id=1, replica_groups=mesh['dom'=64,'grp'=12] {'grp'}, dimensions={0}, use_global_device_ids=true | all-gather | bytes 851968 | tf_op jit(solution)/shard_map/all_gather | solution.py:313
  102.2 1.0 copy-done
  103.2 1.1 copy-done.10
  104.3 19.7 %forward_and_remote_grads.1 = (bf16[256,2048]{1,0:T(8,128)(2,1)S(1)}, bf16[256,2048]{1,0:T(8,128)(2,1)}, bf16[2048,256]{1,0:T(8,128)(2,1)}, bf16[1536,256]{1,0:T(8,128)(2,1)}) custom-call(s32[12]{0:T(128)S(1)} %bitcast.19, bf16[2048,256]{1,0:T(8,128)(2,1)} %bitcast.12, bf16[1536,256]{1,0:T(8,128)(2,1)S(1)} %all_gather.3.fresh_ref, ...), custom_call_target="tpu_custom_call" | custom-call | tf_op jit(solution)/shard_map/forward_and_remote_grads/pallas_call | solution.py:27
  124.1 1.2 copy-done.1
  125.3 1.2 copy-done.8
  126.5 10.5 %own_grads.1 = (f32[2048,256]{1,0:T(8,128)S(1)}, f32[256,256]{1,0:T(8,128)S(1)}, bf16[2048,256]{1,0:T(8,128)(2,1)}) custom-call(bf16[5632,2048]{1,0:T(8,128)(2,1)} %get-tuple-element.16.mixer_ref, bf16[256,2048]{1,0:T(8,128)(2,1)S(1)} %copy-done.8, bf16[256,2048]{1,0:T(8,128)(2,1)S(1)} %get-tuple-element.23.act_ref, bf16[2048,256]{1,0:T(8,128)(2,1)S(1)} %copy-done.3, ...), custom_call_target="tpu_custom_call" | custom-call | flops 2885681152 | bytes 8388608 | tf_op jit(solution)/shard_map/own_grads/pallas_call | solution.py:27
  137.0 1.3 copy-done.4
  138.4 21.6 %all_to_all.25 = f32[64,4,256]{2,1,0:T(4,128)S(1)} all-to-all(f32[64,4,256]{2,1,0:T(4,128)S(1)} %reshape.57), channel_id=1, replica_groups=mesh['dom'=64,'grp'=12] {'dom'}, dimensions={0} | all-to-all | bytes 524288 | tf_op jit(solution)/shard_map/all_to_all | solution.py:429
  160.2 13.6 %all_to_all.26 = f32[12,4,256]{2,1,0:T(4,128)S(1)} all-to-all(f32[12,4,256]{2,1,0:T(4,128)S(1)} %broadcast_in_dim.8), channel_id=1, replica_groups=mesh['dom'=64,'grp'=12] {'grp'}, dimensions={0} | all-to-all | bytes 98304 | tf_op jit(solution)/shard_map/all_to_all | solution.py:433
  173.9 18.1 %all_to_all.27 = f32[64,4,256]{2,1,0:T(4,128)} all-to-all(f32[64,4,256]{2,1,0:T(4,128)S(1)} %broadcast_in_dim.9), channel_id=1, replica_groups=mesh['dom'=64,'grp'=12] {'dom'}, dimensions={0} | all-to-all | bytes 524288 | tf_op jit(solution)/shard_map/all_to_all | solution.py:441
  192.0 6.5 %all-to-all-start.1 = ((bf16[64,32,256]{2,1,0:T(8,128)(2,1)}), bf16[64,32,256]{2,1,0:T(8,128)(2,1)S(1)}, u32[]{:S(2)}, u32[]{:S(2)}) async-start(bf16[64,32,256]{2,1,0:T(8,128)(2,1)} %bitcast.9), calls=%async_computation.1 | async-start | bytes 2097152 | tf_op jit(solution)/shard_map/all_to_all | solution.py:386
  199.4 1.7 reshape.58
  201.2 52.7 %reduce-scatter.2.cloned.1.call-done.owner_ref = bf16[1,128,256]{2,1,0:T(8,128)(2,1)} async-done(((bf16[12,128,256]{2,1,0:T(8,128)(2,1)}), bf16[1,128,256]{2,1,0:T(8,128)(2,1)}) %reduce-scatter.2.cloned.1.call-update) | async-done | bytes 65552 | tf_op jit(solution)/shard_map/reduce_scatter | solution.py:389
  253.9 0.8 copy-done.12
  254.7 5.8 %add_returned_rows.1 = bf16[2048,256]{1,0:T(8,128)(2,1)} custom-call(s32[1,2048]{1,0:T(1,128)S(1)} %reshape.53.send_ref, s32[1,128]{1,0:T(1,128)S(1)} %bitcast.18, f32[2048,256]{1,0:T(8,128)S(1)} %copy-done.5, bf16[2048,256]{1,0:T(8,128)(2,1)S(1)} %bitcast.14, bf16[1,128,256]{2,1,0:T(8,128)(2,1)S(1)} %copy-done.12, bf16[256,256]{1,0:T(8,128)(2,1)S(1)} %copy-done.11), custom_call_target="tpu_custom_call" | custom-call | tf_op jit(solution)/shard_map/add_returned_rows/pallas_call | solution.py:27
  (50 shorter events, 3.2 us)
Async XLA Ops:
  7.2 1.2 copy-start.2
  10.4 17.4 %copy-start.3 = (bf16[2048,256]{1,0:T(8,128)(2,1)S(1)}, bf16[2048,256]{1,0:T(8,128)(2,1)}, u32[]{:S(2)}) copy-start(bf16[2048,256]{1,0:T(8,128)(2,1)} %feat_ref.5) | copy-start | bytes 3145732
  10.4 17.4 %copy-start.11 = (bf16[256,256]{1,0:T(8,128)(2,1)S(1)}, bf16[256,256]{1,0:T(8,128)(2,1)}, u32[]{:S(2)}) copy-start(bf16[256,256]{1,0:T(8,128)(2,1)} %weight_ref.5) | copy-start | bytes 393220
  10.4 17.4 %copy-start.21 = (bf16[1,12,128,256]{3,2,1,0:T(8,128)(2,1)S(1)}, bf16[1,12,128,256]{3,2,1,0:T(8,128)(2,1)}, u32[]{:S(2)}) copy-start(bf16[1,12,128,256]{3,2,1,0:T(8,128)(2,1)} %param.19) | copy-start | bytes 2359300
  10.4 17.4 %copy-start.22 = (s32[2048,8]{0,1:T(8,128)S(1)}, s32[2048,8]{0,1:T(8,128)}, u32[]{:S(2)}) copy-start(s32[2048,8]{0,1:T(8,128)} %param.13) | copy-start | bytes 196612
  10.4 17.4 %copy-start.23 = (f32[2048,8]{0,1:T(8,128)S(1)}, f32[2048,8]{0,1:T(8,128)}, u32[]{:S(2)}) copy-start(f32[2048,8]{0,1:T(8,128)} %param.14) | copy-start | bytes 196612
  14.0 88.2 %all-to-all-start = ((bf16[64,32,256]{2,1,0:T(8,128)(2,1)}), bf16[64,32,256]{2,1,0:T(8,128)(2,1)S(1)}, u32[]{:S(2)}, u32[]{:S(2)}) async-start(bf16[64,32,256]{2,1,0:T(8,128)(2,1)} %bitcast.7), calls=%async_computation | async-start | bytes 2097152 | tf_op jit(solution)/shard_map/all_to_all | solution.py:310
  27.8 1.2 copy-start.20
  29.1 74.1 %copy-start.19 = (s32[1,12]{1,0:T(1,128)S(1)}, s32[1,12]{1,0:T(1,128)}, u32[]{:S(2)}) copy-start(s32[1,12]{1,0:T(1,128)} %param.18) | copy-start | bytes 148
  64.9 1.4 copy-start.6
  66.3 1.0 copy-start.7
  67.3 1.0 copy-start.9
  102.2 1.0 copy-start
  103.2 1.1 copy-start.10
  124.1 1.2 copy-start.1
  125.3 1.2 copy-start.8
  137.0 1.3 copy-start.4
  160.1 39.2 %copy-start.14 = (s32[64,32]{0,1:T(8,128)S(1)}, s32[64,32]{0,1:T(8,128)}, u32[]{:S(2)}) copy-start(s32[64,32]{0,1:T(8,128)} %param.15) | copy-start | bytes 24580
  160.1 39.2 %copy-start.16 = (s32[64]{0:T(128)S(1)}, s32[64]{0:T(128)}, u32[]{:S(2)}) copy-start(s32[64]{0:T(128)} %param.16) | copy-start | bytes 772
  173.9 80.0 %copy-start.5 = (f32[2048,256]{1,0:T(8,128)S(1)}, f32[2048,256]{1,0:T(8,128)}, u32[]{:S(2)}) copy-start(f32[2048,256]{1,0:T(8,128)} %copy-done.4) | copy-start | bytes 6291460
  173.9 80.0 %copy-start.18 = (s32[128]{0:T(128)S(1)}, s32[128]{0:T(128)}, u32[]{:S(2)}) copy-start(s32[128]{0:T(128)} %param.17) | copy-start | bytes 1540
  192.0 61.9 %all-to-all-start.1 = ((bf16[64,32,256]{2,1,0:T(8,128)(2,1)}), bf16[64,32,256]{2,1,0:T(8,128)(2,1)S(1)}, u32[]{:S(2)}, u32[]{:S(2)}) async-start(bf16[64,32,256]{2,1,0:T(8,128)(2,1)} %bitcast.9), calls=%async_computation.1 | async-start | bytes 2097152 | tf_op jit(solution)/shard_map/all_to_all | solution.py:386
  198.5 55.4 %reduce-scatter.2.cloned.1.call-start = ((), (), s32[]{:S(2)}) async-start(), calls=%async_computation.6 | async-start | bytes 851968 | tf_op jit(solution)/shard_map/reduce_scatter | solution.py:389
  253.9 0.8 copy-start.12
  (3 other events, 2.0 us)
Sparse Core Ops, SparseCore 0:
  202.4 51.3 reduce-scatter.1

commit v2 on v0

v2 whole, which is shorter than its diff:
```python
import functools
import math

import jax
import jax.numpy as jnp
from jax import lax
from jax.experimental import pallas as pl
from jax.experimental.pallas import tpu as pltpu
from jax.sharding import PartitionSpec as P

BF16 = jnp.bfloat16
F32 = jnp.float32
BLOCK = 256
LANES = 128
MIB = 1 << 20
PANEL_ROWS = 176
GELU_SCALE = math.sqrt(2.0 / math.pi)
GELU_CUBE = 0.044715


def contract(left, right, left_dim, right_dim):
    return lax.dot_general(
        left, right, (((left_dim,), (right_dim,)), ((), ())), preferred_element_type=F32
    )


def call(kernel, outs, *operands, **options):
    return pl.pallas_call(kernel, out_shape=outs, **options)(*operands)


def shape(dims, dtype):
    return jax.ShapeDtypeStruct(dims, dtype)


VMEM = pl.BlockSpec(memory_space=pltpu.VMEM)
SMEM = pl.BlockSpec(memory_space=pltpu.SMEM)
ANY = pl.BlockSpec(memory_space=pl.ANY)


def small_iota(dims, dim):
    return lax.broadcasted_iota(jnp.int32, dims, dim).astype(jnp.int16)


def one_hot(index, count):
    rows = index.shape[0]
    splat = jnp.broadcast_to(index, (rows, LANES)).astype(jnp.int16)
    lane = small_iota((rows, LANES), 1)
    tiles = []
    for tile in range(count // LANES):
        hit = splat == lane + jnp.int16(tile * LANES)
        tiles.append(jnp.where(hit, jnp.ones((), BF16), jnp.zeros((), BF16)))
    return jnp.concatenate(tiles, axis=1)


def gather_kernel(send_ref, counts_ref, feat_ref, out_ref):
    slots, peers = send_ref.shape
    nodes = feat_ref.shape[0]
    live = lax.broadcasted_iota(jnp.int32, (slots, peers), 0) < counts_ref[...]
    send = jnp.where(live, send_ref[...], -1)
    group = 2 * BLOCK // slots
    for part in range(peers // group):
        index = jnp.concatenate(
            [send[:, peer : peer + 1] for peer in range(part * group, (part + 1) * group)], axis=0
        )
        out_ref[part * 2 * BLOCK : (part + 1) * 2 * BLOCK, :] = jnp.dot(
            one_hot(index, nodes), feat_ref[...], preferred_element_type=F32
        ).astype(BF16)


def panel_kernel(bound_ref, feat_ref, panel_ref):
    nodes = feat_ref.shape[0]
    panel = bound_ref.shape[1]
    bound = jnp.transpose(jnp.broadcast_to(bound_ref[...], (panel, panel)))[:, :1]
    panel_ref[:panel, :] = jnp.dot(
        one_hot(bound, nodes), feat_ref[...], preferred_element_type=F32
    ).astype(BF16)
    panel_ref[panel:, :] = jnp.zeros((panel_ref.shape[0] - panel, feat_ref.shape[1]), BF16)


def build_kernel(
    own_blocks,
    panel_blocks,
    skip_ref,
    index_ref,
    edge_weight_ref,
    feat_ref,
    cached_ref,
    mixer_ref,
    sum_ref,
    stale_ref,
    index_rep,
    weight_rep,
):
    step = pl.program_id(0)
    slots, nodes = index_ref.shape
    wide = 2 * LANES

    @pl.when(step == 0)
    def _():
        index = index_ref[...]
        for slot in range(slots):
            same = index == index[slot : slot + 1]
            merged = jnp.sum(jnp.where(same, edge_weight_ref[...], 0.0), axis=0, keepdims=True)
            index_rep[slot] = jnp.broadcast_to(index[slot : slot + 1], (16, nodes)).astype(
                jnp.int16
            )
            weight_rep[slot] = jnp.broadcast_to(merged, (16, nodes)).astype(BF16)
        sum_ref[...] = jnp.zeros_like(sum_ref)
        stale_ref[...] = jnp.zeros_like(stale_ref)

    row = (lax.broadcasted_iota(jnp.int32, (16, wide), 0) + step * BLOCK).astype(jnp.int16)

    def tile(number, carry):
        lanes = pl.ds(pl.multiple_of(number * wide, wide), wide)
        index = [index_rep[slot, :, lanes] for slot in range(slots)]
        weights = [weight_rep[slot, :, lanes] for slot in range(slots)]
        for start in range(0, BLOCK, 16):
            here = row + jnp.int16(start)
            value = jnp.zeros((16, wide), BF16)
            for slot in range(slots):
                value = jnp.where(index[slot] == here, weights[slot], value)
            mixer_ref[start : start + 16, lanes] = value
        return carry

    lax.fori_loop(0, nodes // wide, tile, 0)

    @pl.when(step < own_blocks)
    def _():
        rows = pl.ds(pl.multiple_of(step * BLOCK, BLOCK), BLOCK)
        sum_ref[...] += contract(mixer_ref[...], feat_ref[rows, :], 0, 0)

    @pl.when(step >= panel_blocks)
    def _():
        panel = cached_ref.shape[0] // skip_ref.shape[0]
        first = (step - panel_blocks) * (BLOCK // panel)
        pieces = []
        for part in range(BLOCK // panel):
            rows = pl.ds(pl.multiple_of((first + part) * panel, panel), panel)
            pieces.append(
                jnp.where(skip_ref[first + part] == 1, cached_ref[rows, :], jnp.zeros((), BF16))
            )
        stale_ref[...] += contract(mixer_ref[...], jnp.concatenate(pieces, axis=0), 0, 0)


def middle_kernel(
    first_row,
    skip_ref,
    arrived_ref,
    fresh_ref,
    weight_ref,
    sum_ref,
    stale_ref,
    cot_ref,
    mixer_ref,
    act_ref,
    grad_ref,
    back_ref,
    panel_ref,
    mixer,
    table,
    sems,
):
    rows, nodes = mixer.shape
    groups = skip_ref.shape[0]
    remote = arrived_ref.shape[0]
    panel = (rows - remote) // groups
    stride = fresh_ref.shape[0] // groups
    width = weight_ref.shape[0]
    peers, peer_rows, _ = back_ref.shape
    slots = remote // peers
    wide = 2 * BLOCK
    blocks = nodes // wide

    def load(number):
        lanes = pl.ds(number * wide, wide)
        return pltpu.make_async_copy(
            mixer_ref.at[pl.ds(first_row, rows), lanes], mixer.at[:, lanes], sems.at[number]
        )

    for number in range(blocks):
        load(number).start()
    table[:remote, :] = arrived_ref[...]
    for group in range(groups):
        table[remote + group * panel : remote + (group + 1) * panel, :] = jnp.where(
            skip_ref[group] == 1,
            jnp.zeros((), BF16),
            fresh_ref[group * stride : group * stride + panel, :],
        )

    term = jnp.zeros((width, width), F32)
    for number in range(blocks):
        load(number).wait()
        here = slice(number * wide, (number + 1) * wide)
        mixed = (sum_ref[here, :] + contract(mixer[:, here], table[...], 0, 0)).astype(BF16)
        x = stale_ref[here, :] + jnp.dot(mixed, weight_ref[...], preferred_element_type=F32)
        square = x * x
        bend = jnp.tanh(GELU_SCALE * x * (1.0 + GELU_CUBE * square))
        half = 0.5 * (1.0 + bend)
        act_ref[here, :] = (x * half).astype(BF16)
        slope = half + (0.5 * GELU_SCALE) * x * (1.0 - bend * bend) * (
            1.0 + (3.0 * GELU_CUBE) * square
        )
        grad = (cot_ref[here, :].astype(F32) * slope).astype(BF16)
        grad_ref[here, :] = grad
        term += contract(mixed, grad, 0, 0)

    high = term.astype(BF16)
    pair = jnp.concatenate([high, (term - high.astype(F32)).astype(BF16)], axis=0)
    share = width // peers
    place = lax.broadcasted_iota(jnp.int32, (2 * width, 2 * width), 0)
    source = lax.broadcasted_iota(jnp.int32, (2 * width, 2 * width), 1)
    peer, offset = place // (2 * share), place % (2 * share)
    wanted = jnp.where(
        offset < share, peer * share + offset, width + peer * share + offset - share
    )
    shares = jnp.dot(
        jnp.where(source == wanted, 1.0, 0.0).astype(BF16), pair, preferred_element_type=F32
    )
    for peer in range(peers):
        back_ref[peer, slots:, :] = shares[peer * 2 * share : (peer + 1) * 2 * share].astype(BF16)

    for start in range(0, remote, wide):
        value = jnp.dot(
            mixer[start : start + wide, :], grad_ref[...], preferred_element_type=F32
        ).astype(BF16)
        for part in range(wide // slots):
            back_ref[start // slots + part, :slots, :] = value[part * slots : (part + 1) * slots]
    for start in range(0, groups * panel, wide):
        value = jnp.dot(
            mixer[remote + start : remote + start + wide, :],
            grad_ref[...],
            preferred_element_type=F32,
        )
        for part in range(wide // panel):
            panel_ref[start + part * panel : start + (part + 1) * panel, :] = jnp.where(
                skip_ref[start // panel + part] == 1,
                0.0,
                value[part * panel : (part + 1) * panel],
            ).astype(BF16)


def local_kernel(mixer_ref, grad_ref, out_ref):
    out_ref[...] = jnp.dot(mixer_ref[...], grad_ref[...], preferred_element_type=F32)


def final_kernel(
    send_ref, bound_ref, local_ref, returned_ref, owner_ref, weight_ref, out_ref, owner_pair
):
    step = pl.program_id(0)
    slots = send_ref.shape[1]
    panel = bound_ref.shape[1]

    @pl.when(step == 0)
    def _():
        total = jnp.sum(owner_ref[...].astype(F32), axis=0)
        high = total.astype(BF16)
        owner_pair[:panel] = high
        owner_pair[panel:] = (total - high.astype(F32)).astype(BF16)

    row = (lax.broadcasted_iota(jnp.int32, (BLOCK, LANES), 0) + step * BLOCK).astype(jnp.int16)

    def columns(ref, start):
        index = jnp.broadcast_to(ref[:, start : start + LANES], (BLOCK, LANES)).astype(jnp.int16)
        return jnp.where(index == row, jnp.ones((), BF16), jnp.zeros((), BF16))

    pick = jnp.concatenate(
        [columns(send_ref, start) for start in range(0, slots, LANES)], axis=1
    )
    pick_owner = jnp.concatenate(
        [columns(bound_ref, start) for start in range(0, panel, LANES)] * 2, axis=1
    )
    total = (
        local_ref[...]
        + jnp.dot(pick, returned_ref[...], preferred_element_type=F32)
        + jnp.dot(pick_owner, owner_pair[...], preferred_element_type=F32)
    )
    out_ref[...] = contract(total.astype(BF16), weight_ref[...], 1, 1).astype(BF16)


def whole(dims):
    return pl.BlockSpec(dims, lambda step: (0,) * len(dims))


def vmem(mib):
    return pltpu.CompilerParams(vmem_limit_bytes=mib * MIB)


def gather_sent(send_rows, counts, features):
    peers, slots = send_rows.shape
    with jax.named_scope("gather_sent_rows"):
        return call(
            gather_kernel,
            shape((peers * slots, features.shape[1]), BF16),
            send_rows.T,
            counts.reshape(1, peers),
            features,
            in_specs=[VMEM] * 3,
            out_specs=VMEM,
            compiler_params=vmem(16),
        )


def gather_panel(bound_row, features, rows):
    with jax.named_scope("gather_panel"):
        return call(
            panel_kernel,
            shape((rows, features.shape[1]), BF16),
            bound_row,
            features,
            in_specs=[VMEM] * 2,
            out_specs=VMEM,
            compiler_params=vmem(8),
        )


def build(skip, edge_index, edge_weight, features, cached, table):
    nodes, width = features.shape
    fanout = edge_index.shape[1]
    with jax.named_scope("build_mixer"):
        return call(
            functools.partial(build_kernel, nodes // BLOCK, (table - cached.shape[0]) // BLOCK),
            (
                shape((table, nodes), BF16),
                shape((nodes, width), F32),
                shape((nodes, width), F32),
            ),
            skip,
            edge_index.T,
            edge_weight.T,
            features,
            cached,
            grid=(table // BLOCK,),
            in_specs=[
                SMEM,
                whole((fanout, nodes)),
                whole((fanout, nodes)),
                whole((nodes, width)),
                whole(cached.shape),
            ],
            out_specs=[
                pl.BlockSpec((BLOCK, nodes), lambda step: (step, 0)),
                whole((nodes, width)),
                whole((nodes, width)),
            ],
            scratch_shapes=[
                pltpu.VMEM((fanout, 16, nodes), jnp.int16),
                pltpu.VMEM((fanout, 16, nodes), BF16),
            ],
            compiler_params=vmem(44),
            cost_estimate=pl.CostEstimate(
                flops=4 * nodes * nodes * width,
                bytes_accessed=2 * table * nodes,
                transcendentals=0,
            ),
        )


def middle(skip, arrived, fresh, weight, own_sum, stale, cotangent, mixer, peers, panel_rows):
    nodes, width = own_sum.shape
    remote = arrived.shape[0]
    others = mixer.shape[0] - nodes
    with jax.named_scope("forward_and_remote_grads"):
        return call(
            functools.partial(middle_kernel, nodes),
            (
                shape((nodes, width), BF16),
                shape((nodes, width), BF16),
                shape((peers, remote // peers + 2 * width // peers, width), BF16),
                shape((panel_rows, width), BF16),
            ),
            skip,
            arrived,
            fresh,
            weight,
            own_sum,
            stale,
            cotangent,
            mixer,
            in_specs=[SMEM] + [VMEM] * 6 + [ANY],
            out_specs=[VMEM] * 4,
            scratch_shapes=[
                pltpu.VMEM((others, nodes), BF16),
                pltpu.VMEM((others, width), BF16),
                pltpu.SemaphoreType.DMA((nodes // (2 * BLOCK),)),
            ],
            compiler_params=vmem(32),
        )


def own_grads(mixer, grad_pre):
    nodes, width = grad_pre.shape
    with jax.named_scope("own_grads"):
        return call(
            local_kernel,
            shape((nodes, width), F32),
            mixer,
            grad_pre,
            grid=(nodes // (2 * BLOCK),),
            in_specs=[
                pl.BlockSpec((2 * BLOCK, nodes), lambda step: (step, 0)),
                whole((nodes, width)),
            ],
            out_specs=pl.BlockSpec((2 * BLOCK, width), lambda step: (step, 0)),
            compiler_params=vmem(44),
            cost_estimate=pl.CostEstimate(
                flops=2 * nodes * nodes * width, bytes_accessed=2 * nodes * nodes, transcendentals=0
            ),
        )


def finish(send_row, bound_row, local_grad, returned, owner_grad, weight):
    nodes, width = local_grad.shape
    panel = bound_row.shape[1]
    with jax.named_scope("add_returned_rows"):
        return call(
            final_kernel,
            shape((nodes, width), BF16),
            send_row,
            bound_row,
            local_grad,
            returned,
            owner_grad,
            weight,
            grid=(nodes // BLOCK,),
            in_specs=[
                whole(send_row.shape),
                whole((1, panel)),
                pl.BlockSpec((BLOCK, width), lambda step: (step, 0)),
                whole(returned.shape),
                whole(owner_grad.shape),
                whole((width, width)),
            ],
            out_specs=pl.BlockSpec((BLOCK, width), lambda step: (step, 0)),
            scratch_shapes=[pltpu.VMEM((2 * panel, width), BF16)],
            compiler_params=vmem(16),
        )


def exchange(values, axis):
    return lax.all_to_all(values, axis, split_axis=0, concat_axis=0, tiled=True)


def everyone(part, axis):
    return exchange(jnp.broadcast_to(part[None], (lax.axis_size(axis),) + part.shape), axis)


def shards(
    features,
    weight,
    cotangent,
    edge_index,
    edge_weight,
    send_rows,
    counts,
    boundary,
    skip_flags,
    cached_panels,
):
    nodes, width = features.shape
    peers = lax.axis_size("dom")
    groups = lax.axis_size("grp")
    slots = send_rows.shape[1]
    panel = boundary.shape[0]
    remote = peers * slots
    table = nodes + remote + groups * panel
    bound_row = boundary.reshape(1, panel)
    skip = skip_flags.reshape(groups)

    own_panel = gather_panel(bound_row, features, PANEL_ROWS)
    fresh = lax.all_gather(own_panel, "grp", axis=0, tiled=True)
    outgoing = gather_sent(send_rows, counts, features)
    arrived = exchange(outgoing.reshape(peers, slots, width), "dom").reshape(remote, width)
    mixer, own_sum, stale = build(
        skip,
        edge_index,
        edge_weight,
        features,
        cached_panels.reshape(groups * panel, width),
        table,
    )
    activated, grad_pre, back, panel_grad = middle(
        skip, arrived, fresh, weight, own_sum, stale, cotangent, mixer, peers, groups * panel
    )
    owner_grad = lax.psum_scatter(
        panel_grad.reshape(groups, panel, width), "grp", scatter_dimension=0, tiled=True
    )
    returned = exchange(back, "dom")
    local_grad = own_grads(mixer, grad_pre)
    returned, local_grad = lax.optimization_barrier((returned, local_grad))

    share = width // peers
    pairs = returned[:, slots:, :].astype(F32)
    part = jnp.sum(pairs[:, :share] + pairs[:, share:], axis=0)
    part = jnp.sum(everyone(part, "grp"), axis=0) * (1.0 / math.sqrt(nodes * peers * groups))
    weight_grad = everyone(part, "dom").reshape(width, width)

    live = lax.broadcasted_iota(jnp.int32, send_rows.shape, 1) < counts[:, None]
    send_row = jnp.pad(
        jnp.where(live, send_rows, -1), ((0, 0), (0, 2 * share)), constant_values=-1
    ).reshape(1, peers * (slots + 2 * share))
    feature_grad = finish(
        send_row, bound_row, local_grad, returned.reshape(-1, width), owner_grad, weight
    )
    return (activated, feature_grad, weight_grad)


def solution(mesh):
    in_specs = (
        P(("dom", "grp"), None),
        P(),
        P(("dom", "grp"), None),
        P(("dom", "grp"), None),
        P(("dom", "grp"), None),
        P(("dom", "grp"), None),
        P(("dom", "grp")),
        P(("dom", "grp")),
        P("dom", None),
        P("dom", None, None, None),
    )
    out_specs = (P(("dom", "grp"), None), P(("dom", "grp"), None), P())
    return jax.shard_map(shards, mesh=mesh, in_specs=in_specs, out_specs=out_specs, check_vma=False)
```

time: 842 us -> 213 us (0.25)
  waiting for transfers between devices: 498 us -> 56.2 us
  other arithmetic: 166 us -> 3.51 us
  local copies, waits for them, and re-layouts: 98.5 us -> 21.8 us
  Pallas kernels: 0 us -> 60.9 us
  blocking collectives: 29.5 us -> 14.9 us
  starting transfers between devices: 30.4 us -> 40.3 us
    psum x1 -> x0, waiting for transfers between devices: 470 us -> none  [shards(): lax.psum(weight_term, ('dom', 'grp')) * (1.0 / math.sqrt(total_nodes))]
    scatter-add x6 -> x0, other arithmetic: 133 us -> none  [the longest x4 118 us: add_block(): running.at[index_block.reshape(-1)].add(contrib.reshape(-1, hidden_width))]
    gather x6 -> x0, local copies, waits for them, and re-layouts: 69.1 us -> none  [the longest x4 60.7 us: one_block(): picked = source_table[index_block]]
    pallas_call x0 -> x6, Pallas kernels: none -> 60.9 us  [call(): return pl.pallas_call(kernel, out_shape=outs, **options)(*operands)]
    all_gather x1 -> x0, blocking collectives: 29.5 us -> none  [shards(): fresh = lax.all_gather(projected[boundary][None], 'grp', axis=0, tiled=True)]
    all_gather x0 -> x1, waiting for transfers between devices: none -> 28.8 us  [shards(): fresh = lax.all_gather(own_panel, 'grp', axis=0, tiled=True)]
    all_to_all x0 -> x1, blocking collectives: none -> 14.9 us  [exchange(): return lax.all_to_all(values, axis, split_axis=0, concat_axis=0, tiled=True)]
    unnamed x18 -> x45, local copies, waits for them, and re-layouts: 3.6 us -> 17.1 us
  transfers between devices with their start and end apart: 4 -> 5, of which waited for: 3 -> 2; matrix products, arithmetic and copies ran while one was open for 3% -> 4% of each run, Pallas kernels for 0% -> 18%
where the time goes in v2:
time: 213 us; the launch traced here: 212 us
  Pallas kernels  60.9 us (29%)
  waiting for transfers between devices  56.2 us (26%)
  starting transfers between devices  40.3 us (19%)
  local copies, waits for them, and re-layouts  21.8 us (10%)
  blocking collectives  14.9 us (7%)
  between operations  14.2 us (7%)
  other arithmetic  3.51 us (2%)
    pallas_call x6, Pallas kernels, call(): return pl.pallas_call(kernel, out_shape=outs, **options)(*operands)  60.9 us
    all_to_all x3, starting transfers between devices, exchange(): return lax.all_to_all(values, axis, split_axis=0, concat_axis=0, tiled=True)  40.2 us
    all_gather x1, waiting for transfers between devices, shards(): fresh = lax.all_gather(own_panel, 'grp', axis=0, tiled=True)  28.8 us
    all_to_all x3, waiting for transfers between devices, exchange(): return lax.all_to_all(values, axis, split_axis=0, concat_axis=0, tiled=True)  26.7 us
    unnamed x45, local copies, waits for them, and re-layouts  17.1 us
    all_to_all x1, blocking collectives, exchange(): return lax.all_to_all(values, axis, split_axis=0, concat_axis=0, tiled=True)  14.9 us
  transfers between devices with their start and end apart: 5, of which 2 were waited for; matrix products, arithmetic and copies ran while one was open for 4% of the time, Pallas kernels for 18%

profile of v2, /device:TPU:1, one launch (start us, length us, event | category | flops | bytes accessed | tf_op | source)
XLA Modules:
  0.0 211.8 jit_solution(11579625193220563418)
XLA Ops:
  7.2 1.2 copy-done
  9.8 3.5 %gather_sent_rows.1 = bf16[2048,256]{1,0:T(8,128)(2,1)} custom-call(s32[32,64]{1,0:T(8,128)S(1)} %bitcast.13, s32[1,64]{1,0:T(1,128)S(1)} %bitcast.14, bf16[2048,256]{1,0:T(8,128)(2,1)S(1)} %copy-done), custom_call_target="tpu_custom_call" | custom-call | tf_op jit(solution)/shard_map/gather_sent_rows/pallas_call | solution.py:28
  13.3 14.7 %all-to-all-start = ((bf16[64,32,256]{2,1,0:T(8,128)(2,1)}), bf16[64,32,256]{2,1,0:T(8,128)(2,1)S(1)}, u32[]{:S(2)}, u32[]{:S(2)}) async-start(bf16[64,32,256]{2,1,0:T(8,128)(2,1)} %bitcast.3), calls=%async_computation | async-start | bytes 2097152 | tf_op jit(solution)/shard_map/all_to_all | solution.py:440
  29.2 1.1 copy-done.19
  30.4 26.2 %build_mixer.1 = (bf16[5632,2048]{1,0:T(8,128)(2,1)}, f32[2048,256]{1,0:T(8,128)S(1)}, f32[2048,256]{1,0:T(8,128)S(1)}) custom-call(s32[12]{0:T(128)S(1)} %bitcast.17, s32[8,2048]{1,0:T(8,128)S(1)} %bitcast.20, f32[8,2048]{1,0:T(8,128)S(1)} %bitcast.21, bf16[2048,256]{1,0:T(8,128)(2,1)S(1)} %copy-done.1, bf16[1536,256]{1,0:T(8,128)(2,1)S(1)} %bitcast.19), custom_call_target="tpu_custom_call" | custom-call | flops 4294967296 | bytes 23068672 | tf_op jit(solution)/shard_map/build_mixer/pallas_call | solution.py:28
  56.6 1.4 copy-done.2
  57.9 1.4 copy-done.4
  59.3 28.8 %all-gather.2.cloned.1.call-done.fresh_ref = bf16[2112,256]{1,0:T(8,128)(2,1)} async-done(((bf16[176,256]{1,0:T(8,128)(2,1)}), bf16[2112,256]{1,0:T(8,128)(2,1)}) %all-gather.2.cloned.1.call-update) | async-done | bytes 1081360 | tf_op jit(solution)/shard_map/all_gather | solution.py:470
  88.2 1.6 copy-done.3
  89.8 1.6 copy-done.5
  91.3 1.2 copy-done.7
  92.6 18.3 %forward_and_remote_grads.1 = (bf16[2048,256]{1,0:T(8,128)(2,1)}, bf16[2048,256]{1,0:T(8,128)(2,1)S(1)}, bf16[64,40,256]{2,1,0:T(8,128)(2,1)S(1)}, bf16[1536,256]{1,0:T(8,128)(2,1)}) custom-call(s32[12]{0:T(128)S(1)} %bitcast.18, bf16[2048,256]{1,0:T(8,128)(2,1)S(1)} %bitcast.12, bf16[2112,256]{1,0:T(8,128)(2,1)S(1)} %copy-done.7, ...), custom_call_target="tpu_custom_call" | custom-call | tf_op jit(solution)/shard_map/forward_and_remote_grads/pallas_call | solution.py:28
  112.9 17.2 %all-to-all-start.1 = ((bf16[64,40,256]{2,1,0:T(8,128)(2,1)}), bf16[64,40,256]{2,1,0:T(8,128)(2,1)S(1)}, u32[]{:S(2)}, u32[]{:S(2)}) async-start(bf16[64,40,256]{2,1,0:T(8,128)(2,1)} %copy-done.6), calls=%async_computation.1 | async-start | bytes 2621440 | tf_op jit(solution)/shard_map/all_to_all | solution.py:440
  130.9 1.2 copy-done.10
  132.1 5.5 %own_grads.1.local_ref = f32[2048,256]{1,0:T(8,128)S(1)} custom-call(bf16[5632,2048]{1,0:T(8,128)(2,1)} %get-tuple-element.14.mixer_ref, bf16[2048,256]{1,0:T(8,128)(2,1)S(1)} %copy-done.10), custom_call_target="tpu_custom_call" | custom-call | flops 2147483648 | bytes 8388608 | tf_op jit(solution)/shard_map/own_grads/pallas_call | solution.py:28
  137.6 26.7 %all-to-all-done.1 = bf16[64,40,256]{2,1,0:T(8,128)(2,1)S(1)} async-done(((bf16[64,40,256]{2,1,0:T(8,128)(2,1)}), bf16[64,40,256]{2,1,0:T(8,128)(2,1)S(1)}, u32[]{:S(2)}, u32[]{:S(2)}) %all-to-all-start.1) | async-done | bytes 1310752 | tf_op jit(solution)/shard_map/all_to_all | solution.py:440
  164.5 14.9 %all_to_all.20 = f32[12,4,256]{2,1,0:T(4,128)} all-to-all(f32[12,4,256]{2,1,0:T(4,128)S(1)} %broadcast_in_dim.8), channel_id=1, replica_groups=mesh['dom'=64,'grp'=12] {'grp'}, dimensions={0} | all-to-all | bytes 98304 | tf_op jit(solution)/shard_map/all_to_all | solution.py:440
  179.4 1.4 reduce_sum.19
  182.2 8.3 %all-to-all-start.3 = ((f32[64,4,256]{2,1,0:T(4,128)}), f32[64,4,256]{2,1,0:T(4,128)}, u32[]{:S(2)}, u32[]{:S(2)}) async-start(f32[64,4,256]{2,1,0:T(4,128)} %broadcast_in_dim.9), calls=%async_computation.4 | async-start | bytes 524288 | tf_op jit(solution)/shard_map/all_to_all | solution.py:440
  190.5 1.3 fusion.1
  191.8 1.4 copy.16
  193.2 1.4 pad.4.clone
  196.9 6.3 %add_returned_rows.1 = bf16[2048,256]{1,0:T(8,128)(2,1)} custom-call(s32[1,2560]{1,0:T(1,128)S(1)} %reshape.47.send_ref, s32[1,128]{1,0:T(1,128)S(1)} %bitcast.16, f32[2048,256]{1,0:T(8,128)S(1)} %own_grads.1.local_ref, bf16[2560,256]{1,0:T(8,128)(2,1)S(1)} %bitcast.11, bf16[1,128,256]{2,1,0:T(8,128)(2,1)S(1)} %copy-done.12, bf16[256,256]{1,0:T(8,128)(2,1)S(1)} %copy-done.11), custom_call_target="tpu_custom_call" | custom-call | tf_op jit(solution)/shard_map/add_returned_rows/pallas_call | solution.py:28
  203.2 1.7 reshape.50
  (50 shorter events, 9.3 us)
Async XLA Ops:
  7.2 1.2 copy-start
  9.8 18.3 %copy-start.1 = (bf16[2048,256]{1,0:T(8,128)(2,1)S(1)}, bf16[2048,256]{1,0:T(8,128)(2,1)}, u32[]{:S(2)}) copy-start(bf16[2048,256]{1,0:T(8,128)(2,1)} %feat_ref.5) | copy-start | bytes 3145732
  9.8 18.3 %copy-start.16 = (s32[128]{0:T(128)S(1)}, s32[128]{0:T(128)}, u32[]{:S(2)}) copy-start(s32[128]{0:T(128)} %param.17) | copy-start | bytes 1540
  13.3 15.9 %copy-start.18 = (s32[1,12]{1,0:T(1,128)S(1)}, s32[1,12]{1,0:T(1,128)}, u32[]{:S(2)}) copy-start(s32[1,12]{1,0:T(1,128)} %param.18) | copy-start | bytes 148
  13.3 15.9 %copy-start.20 = (s32[2048,8]{0,1:T(8,128)S(1)}, s32[2048,8]{0,1:T(8,128)}, u32[]{:S(2)}) copy-start(s32[2048,8]{0,1:T(8,128)} %param.13) | copy-start | bytes 196612
  13.3 15.9 %copy-start.21 = (f32[2048,8]{0,1:T(8,128)S(1)}, f32[2048,8]{0,1:T(8,128)}, u32[]{:S(2)}) copy-start(f32[2048,8]{0,1:T(8,128)} %param.14) | copy-start | bytes 196612
  13.3 74.8 %all-to-all-start = ((bf16[64,32,256]{2,1,0:T(8,128)(2,1)}), bf16[64,32,256]{2,1,0:T(8,128)(2,1)S(1)}, u32[]{:S(2)}, u32[]{:S(2)}) async-start(bf16[64,32,256]{2,1,0:T(8,128)(2,1)} %bitcast.3), calls=%async_computation | async-start | bytes 2097152 | tf_op jit(solution)/shard_map/all_to_all | solution.py:440
  28.1 60.1 %all-gather.2.cloned.1.call-start = ((), (), s32[]{:S(2)}) async-start(), calls=%async_computation.5 | async-start | bytes 1171456 | tf_op jit(solution)/shard_map/all_gather | solution.py:470
  29.2 1.1 copy-start.19
  30.4 57.8 %copy-start.8 = (bf16[2048,256]{1,0:T(8,128)(2,1)S(1)}, bf16[2048,256]{1,0:T(8,128)(2,1)}, u32[]{:S(2)}) copy-start(bf16[2048,256]{1,0:T(8,128)(2,1)} %cot_ref.1) | copy-start | bytes 3145732
  30.4 57.8 %copy-start.11 = (bf16[256,256]{1,0:T(8,128)(2,1)S(1)}, bf16[256,256]{1,0:T(8,128)(2,1)}, u32[]{:S(2)}) copy-start(bf16[256,256]{1,0:T(8,128)(2,1)} %weight_ref.3) | copy-start | bytes 393220
  56.6 1.4 copy-start.2
  57.9 1.4 copy-start.4
  88.2 1.6 copy-start.3
  89.7 1.6 copy-start.5
  91.3 1.2 copy-start.7
  110.9 1.1 copy-start.6
  111.9 1.0 copy-start.9
  112.9 51.4 %all-to-all-start.1 = ((bf16[64,40,256]{2,1,0:T(8,128)(2,1)}), bf16[64,40,256]{2,1,0:T(8,128)(2,1)S(1)}, u32[]{:S(2)}, u32[]{:S(2)}) async-start(bf16[64,40,256]{2,1,0:T(8,128)(2,1)} %copy-done.6), calls=%async_computation.1 | async-start | bytes 2621440 | tf_op jit(solution)/shard_map/all_to_all | solution.py:440
  130.1 65.3 %reduce-scatter.2.cloned.1.call-start = ((), (), s32[]{:S(2)}) async-start(), calls=%async_computation.6 | async-start | bytes 851968 | tf_op jit(solution)/shard_map/reduce_scatter | solution.py:484
  130.9 1.2 copy-start.10
  137.6 52.9 %copy-start.14 = (s32[64,32]{0,1:T(8,128)S(1)}, s32[64,32]{0,1:T(8,128)}, u32[]{:S(2)}) copy-start(s32[64,32]{0,1:T(8,128)} %param.15) | copy-start | bytes 24580
  182.2 21.0 %all-to-all-start.3 = ((f32[64,4,256]{2,1,0:T(4,128)}), f32[64,4,256]{2,1,0:T(4,128)}, u32[]{:S(2)}, u32[]{:S(2)}) async-start(f32[64,4,256]{2,1,0:T(4,128)} %broadcast_in_dim.9), calls=%async_computation.4 | async-start | bytes 524288 | tf_op jit(solution)/shard_map/all_to_all | solution.py:440
  195.4 0.8 copy-start.12
  (3 other events, 2.0 us)
Sparse Core Ops, SparseCore 0:
  31.9 56.2 all-gather.1
  134.1 48.3 reduce-scatter.1

commit v3 on v2

--- a/solution.py
+++ b/solution.py
@@ -13,7 +13,6 @@
 BLOCK = 256
 LANES = 128
 MIB = 1 << 20
-PANEL_ROWS = 176
 GELU_SCALE = math.sqrt(2.0 / math.pi)
 GELU_CUBE = 0.044715
 
@@ -71,10 +70,9 @@
     nodes = feat_ref.shape[0]
     panel = bound_ref.shape[1]
     bound = jnp.transpose(jnp.broadcast_to(bound_ref[...], (panel, panel)))[:, :1]
-    panel_ref[:panel, :] = jnp.dot(
+    panel_ref[...] = jnp.dot(
         one_hot(bound, nodes), feat_ref[...], preferred_element_type=F32
     ).astype(BF16)
-    panel_ref[panel:, :] = jnp.zeros((panel_ref.shape[0] - panel, feat_ref.shape[1]), BF16)
 
 
 def build_kernel(
@@ -145,9 +143,9 @@
 def middle_kernel(
     first_row,
     skip_ref,
+    weight_ref,
     arrived_ref,
     fresh_ref,
-    weight_ref,
     sum_ref,
     stale_ref,
     cot_ref,
@@ -158,15 +156,22 @@
     panel_ref,
     mixer,
     table,
-    sems,
+    own_sum,
+    stale,
+    cot,
+    act,
+    grad,
+    back,
+    panel_back,
+    in_sems,
+    block_sems,
+    out_sems,
 ):
     rows, nodes = mixer.shape
     groups = skip_ref.shape[0]
-    remote = arrived_ref.shape[0]
+    remote, width = arrived_ref.shape
     panel = (rows - remote) // groups
-    stride = fresh_ref.shape[0] // groups
-    width = weight_ref.shape[0]
-    peers, peer_rows, _ = back_ref.shape
+    peers, peer_rows, _ = back.shape
     slots = remote // peers
     wide = 2 * BLOCK
     blocks = nodes // wide
@@ -174,69 +179,107 @@
     def load(number):
         lanes = pl.ds(number * wide, wide)
         return pltpu.make_async_copy(
-            mixer_ref.at[pl.ds(first_row, rows), lanes], mixer.at[:, lanes], sems.at[number]
-        )
-
-    for number in range(blocks):
+            mixer_ref.at[pl.ds(first_row, rows), lanes], mixer.at[:, lanes], block_sems.at[number]
+        )
+
+    fetches = [
+        pltpu.make_async_copy(source, target, in_sems.at[number])
+        for number, (source, target) in enumerate(
+            (
+                (arrived_ref, table.at[pl.ds(0, remote)]),
+                (fresh_ref, table.at[pl.ds(remote, groups * panel)]),
+                (sum_ref, own_sum),
+                (stale_ref, stale),
+                (cot_ref, cot),
+            )
+        )
+    ]
+    for fetch in fetches[:2]:
+        fetch.start()
+    load(0).start()
+    for fetch in fetches[2:]:
+        fetch.start()
+    for number in range(1, blocks):
         load(number).start()
-    table[:remote, :] = arrived_ref[...]
+    for fetch in fetches[:2]:
+        fetch.wait()
     for group in range(groups):
-        table[remote + group * panel : remote + (group + 1) * panel, :] = jnp.where(
-            skip_ref[group] == 1,
-            jnp.zeros((), BF16),
-            fresh_ref[group * stride : group * stride + panel, :],
-        )
+        here = slice(remote + group * panel, remote + (group + 1) * panel)
+        table[here, :] = jnp.where(skip_ref[group] == 1, jnp.zeros((), BF16), table[here, :])
 
     term = jnp.zeros((width, width), F32)
     for number in range(blocks):
         load(number).wait()
         here = slice(number * wide, (number + 1) * wide)
-        mixed = (sum_ref[here, :] + contract(mixer[:, here], table[...], 0, 0)).astype(BF16)
-        x = stale_ref[here, :] + jnp.dot(mixed, weight_ref[...], preferred_element_type=F32)
+        product = contract(mixer[:, here], table[...], 0, 0)
+        if number == 0:
+            for fetch in fetches[2:]:
+                fetch.wait()
+        mixed = (own_sum[here, :] + product).astype(BF16)
+        x = stale[here, :] + jnp.dot(mixed, weight_ref[...], preferred_element_type=F32)
         square = x * x
         bend = jnp.tanh(GELU_SCALE * x * (1.0 + GELU_CUBE * square))
         half = 0.5 * (1.0 + bend)
-        act_ref[here, :] = (x * half).astype(BF16)
+        act[here, :] = (x * half).astype(BF16)
         slope = half + (0.5 * GELU_SCALE) * x * (1.0 - bend * bend) * (
             1.0 + (3.0 * GELU_CUBE) * square
         )
-        grad = (cot_ref[here, :].astype(F32) * slope).astype(BF16)
-        grad_ref[here, :] = grad
-        term += contract(mixed, grad, 0, 0)
+        part = (cot[here, :].astype(F32) * slope).astype(BF16)
+        grad[here, :] = part
+        term += contract(mixed, part, 0, 0)
+
+    out_copies = [
+        pltpu.make_async_copy(act, act_ref, out_sems.at[0]),
+        pltpu.make_async_copy(grad, grad_ref, out_sems.at[1]),
+    ]
+    for copy in out_copies:
+        copy.start()
 
     high = term.astype(BF16)
-    pair = jnp.concatenate([high, (term - high.astype(F32)).astype(BF16)], axis=0)
-    share = width // peers
-    place = lax.broadcasted_iota(jnp.int32, (2 * width, 2 * width), 0)
-    source = lax.broadcasted_iota(jnp.int32, (2 * width, 2 * width), 1)
-    peer, offset = place // (2 * share), place % (2 * share)
-    wanted = jnp.where(
-        offset < share, peer * share + offset, width + peer * share + offset - share
-    )
-    shares = jnp.dot(
-        jnp.where(source == wanted, 1.0, 0.0).astype(BF16), pair, preferred_element_type=F32
-    )
+    low = (term - high.astype(F32)).astype(BF16)
+    across = width // LANES
+    tall = width * across // peers
     for peer in range(peers):
-        back_ref[peer, slots:, :] = shares[peer * 2 * share : (peer + 1) * 2 * share].astype(BF16)
-
-    for start in range(0, remote, wide):
+        place = (
+            slice(peer // across * tall, (peer // across + 1) * tall),
+            slice(peer % across * LANES, (peer % across + 1) * LANES),
+        )
+        back[peer, slots:, :LANES] = high[place]
+        back[peer, slots:, LANES:] = low[place]
+
+    tall_block = remote // 2
+    for start in range(0, remote, tall_block):
         value = jnp.dot(
-            mixer[start : start + wide, :], grad_ref[...], preferred_element_type=F32
+            mixer[start : start + tall_block, :], grad[...], preferred_element_type=F32
         ).astype(BF16)
-        for part in range(wide // slots):
-            back_ref[start // slots + part, :slots, :] = value[part * slots : (part + 1) * slots]
-    for start in range(0, groups * panel, wide):
+        first = start // slots
+        count = tall_block // slots
+        for part in range(count):
+            back[first + part, :slots, :] = value[part * slots : (part + 1) * slots]
+        copy = pltpu.make_async_copy(
+            back.at[pl.ds(first, count)],
+            back_ref.at[pl.ds(first, count)],
+            out_sems.at[2 + start // tall_block],
+        )
+        copy.start()
+        out_copies.append(copy)
+    tall_block = groups * panel // 2
+    for start in range(0, groups * panel, tall_block):
         value = jnp.dot(
-            mixer[remote + start : remote + start + wide, :],
-            grad_ref[...],
+            mixer[remote + start : remote + start + tall_block, :],
+            grad[...],
             preferred_element_type=F32,
         )
-        for part in range(wide // panel):
-            panel_ref[start + part * panel : start + (part + 1) * panel, :] = jnp.where(
+        for part in range(tall_block // panel):
+            panel_back[start + part * panel : start + (part + 1) * panel, :] = jnp.where(
                 skip_ref[start // panel + part] == 1,
                 0.0,
                 value[part * panel : (part + 1) * panel],
             ).astype(BF16)
+    copy = pltpu.make_async_copy(panel_back, panel_ref, out_sems.at[4])
+    copy.start()
+    for copy in out_copies + [copy]:
+        copy.wait()
 
 
 def local_kernel(mixer_ref, grad_ref, out_ref):
@@ -300,11 +343,11 @@
         )
 
 
-def gather_panel(bound_row, features, rows):
+def gather_panel(bound_row, features):
     with jax.named_scope("gather_panel"):
         return call(
             panel_kernel,
-            shape((rows, features.shape[1]), BF16),
+            shape((bound_row.shape[1], features.shape[1]), BF16),
             bound_row,
             features,
             in_specs=[VMEM] * 2,
@@ -359,31 +402,41 @@
     nodes, width = own_sum.shape
     remote = arrived.shape[0]
     others = mixer.shape[0] - nodes
+    back = (peers, remote // peers + width * width // (peers * LANES), width)
     with jax.named_scope("forward_and_remote_grads"):
         return call(
             functools.partial(middle_kernel, nodes),
             (
                 shape((nodes, width), BF16),
                 shape((nodes, width), BF16),
-                shape((peers, remote // peers + 2 * width // peers, width), BF16),
+                shape(back, BF16),
                 shape((panel_rows, width), BF16),
             ),
             skip,
+            weight,
             arrived,
             fresh,
-            weight,
             own_sum,
             stale,
             cotangent,
             mixer,
-            in_specs=[SMEM] + [VMEM] * 6 + [ANY],
-            out_specs=[VMEM] * 4,
+            in_specs=[SMEM, VMEM] + [ANY] * 6,
+            out_specs=[ANY] * 4,
             scratch_shapes=[
                 pltpu.VMEM((others, nodes), BF16),
                 pltpu.VMEM((others, width), BF16),
+                pltpu.VMEM((nodes, width), F32),
+                pltpu.VMEM((nodes, width), F32),
+                pltpu.VMEM((nodes, width), BF16),
+                pltpu.VMEM((nodes, width), BF16),
+                pltpu.VMEM((nodes, width), BF16),
+                pltpu.VMEM(back, BF16),
+                pltpu.VMEM((panel_rows, width), BF16),
+                pltpu.SemaphoreType.DMA((5,)),
                 pltpu.SemaphoreType.DMA((nodes // (2 * BLOCK),)),
+                pltpu.SemaphoreType.DMA((5,)),
             ],
-            compiler_params=vmem(32),
+            compiler_params=vmem(56),
         )
 
 
@@ -466,8 +519,9 @@
     bound_row = boundary.reshape(1, panel)
     skip = skip_flags.reshape(groups)
 
-    own_panel = gather_panel(bound_row, features, PANEL_ROWS)
+    own_panel = gather_panel(bound_row, features)
     fresh = lax.all_gather(own_panel, "grp", axis=0, tiled=True)
+    skip, fresh = lax.optimization_barrier((skip, fresh))
     outgoing = gather_sent(send_rows, counts, features)
     arrived = exchange(outgoing.reshape(peers, slots, width), "dom").reshape(remote, width)
     mixer, own_sum, stale = build(
@@ -488,16 +542,22 @@
     local_grad = own_grads(mixer, grad_pre)
     returned, local_grad = lax.optimization_barrier((returned, local_grad))
 
-    share = width // peers
     pairs = returned[:, slots:, :].astype(F32)
-    part = jnp.sum(pairs[:, :share] + pairs[:, share:], axis=0)
+    part = jnp.sum(pairs[:, :, :LANES] + pairs[:, :, LANES:], axis=0)
     part = jnp.sum(everyone(part, "grp"), axis=0) * (1.0 / math.sqrt(nodes * peers * groups))
-    weight_grad = everyone(part, "dom").reshape(width, width)
+    across = width // LANES
+    tall = part.shape[0]
+    weight_grad = (
+        everyone(part, "dom")
+        .reshape(peers // across, across, tall, LANES)
+        .transpose(0, 2, 1, 3)
+        .reshape(width, width)
+    )
 
     live = lax.broadcasted_iota(jnp.int32, send_rows.shape, 1) < counts[:, None]
     send_row = jnp.pad(
-        jnp.where(live, send_rows, -1), ((0, 0), (0, 2 * share)), constant_values=-1
-    ).reshape(1, peers * (slots + 2 * share))
+        jnp.where(live, send_rows, -1), ((0, 0), (0, tall)), constant_values=-1
+    ).reshape(1, peers * (slots + tall))
     feature_grad = finish(
         send_row, bound_row, local_grad, returned.reshape(-1, width), owner_grad, weight
     )

time: 213 us -> 205 us (0.962)
  waiting for transfers between devices: 56.2 us -> 27.4 us
  blocking collectives: 14.9 us -> 43.3 us
  local copies, waits for them, and re-layouts: 21.8 us -> 15.1 us
    all_gather x0 -> x1, blocking collectives: none -> 30.6 us  [shards(): fresh = lax.all_gather(own_panel, 'grp', axis=0, tiled=True)]
    all_gather x1 -> x0, waiting for transfers between devices: 28.8 us -> none  [shards(): fresh = lax.all_gather(own_panel, 'grp', axis=0, tiled=True)]
    unnamed x45 -> x36, local copies, waits for them, and re-layouts: 17.1 us -> 12.1 us
    all_to_all x1, blocking collectives: 14.9 us -> 12.7 us  [exchange(): return lax.all_to_all(values, axis, split_axis=0, concat_axis=0, tiled=True)]
  transfers between devices with their start and end apart: 5 -> 4, of which waited for: 2 -> 1; matrix products, arithmetic and copies ran while one was open for 4% -> 4% of each run, Pallas kernels for 18% -> 19%
where the time goes in v3:
time: 205 us; the launch traced here: 204 us
  Pallas kernels  62 us (30%)
  blocking collectives  43.3 us (21%)
  starting transfers between devices  38.3 us (19%)
  waiting for transfers between devices  27.4 us (13%)
  local copies, waits for them, and re-layouts  15.1 us (7%)
  between operations  14.2 us (7%)
  other arithmetic  3.46 us (2%)
    pallas_call x6, Pallas kernels, call(): return pl.pallas_call(kernel, out_shape=outs, **options)(*operands)  62 us
    all_to_all x3, starting transfers between devices, exchange(): return lax.all_to_all(values, axis, split_axis=0, concat_axis=0, tiled=True)  38.2 us
    all_gather x1, blocking collectives, shards(): fresh = lax.all_gather(own_panel, 'grp', axis=0, tiled=True)  30.6 us
    all_to_all x3, waiting for transfers between devices, exchange(): return lax.all_to_all(values, axis, split_axis=0, concat_axis=0, tiled=True)  26.7 us
    all_to_all x1, blocking collectives, exchange(): return lax.all_to_all(values, axis, split_axis=0, concat_axis=0, tiled=True)  12.7 us
    unnamed x36, local copies, waits for them, and re-layouts  12.1 us
  transfers between devices with their start and end apart: 4, of which 1 were waited for; matrix products, arithmetic and copies ran while one was open for 4% of the time, Pallas kernels for 19%

profile of v3, /device:TPU:1, one launch (start us, length us, event | category | flops | bytes accessed | tf_op | source)
XLA Modules:
  0.0 203.7 jit_solution(14022741195665497384)
XLA Ops:
  7.2 1.2 copy-done
  9.8 3.5 %gather_sent_rows.1 = bf16[2048,256]{1,0:T(8,128)(2,1)} custom-call(s32[32,64]{1,0:T(8,128)S(1)} %bitcast.17, s32[1,64]{1,0:T(1,128)S(1)} %bitcast.18, bf16[2048,256]{1,0:T(8,128)(2,1)S(1)} %copy-done), custom_call_target="tpu_custom_call" | custom-call | tf_op jit(solution)/shard_map/gather_sent_rows/pallas_call | solution.py:27
  13.3 14.7 %all-to-all-start = ((bf16[64,32,256]{2,1,0:T(8,128)(2,1)}), bf16[64,32,256]{2,1,0:T(8,128)(2,1)S(1)}, u32[]{:S(2)}, u32[]{:S(2)}) async-start(bf16[64,32,256]{2,1,0:T(8,128)(2,1)} %bitcast.4), calls=%async_computation | async-start | bytes 2097152 | tf_op jit(solution)/shard_map/all_to_all | solution.py:493
  28.5 30.6 %all_gather.3.fresh_ref = bf16[1536,256]{1,0:T(8,128)(2,1)} all-gather(bf16[128,256]{1,0:T(8,128)(2,1)S(1)} %gather_panel.1), channel_id=1, replica_groups=mesh['dom'=64,'grp'=12] {'grp'}, dimensions={0}, use_global_device_ids=true | all-gather | bytes 851968 | tf_op jit(solution)/shard_map/all_gather | solution.py:523
  59.1 26.0 %build_mixer.1 = (bf16[5632,2048]{1,0:T(8,128)(2,1)}, f32[2048,256]{1,0:T(8,128)S(1)}, f32[2048,256]{1,0:T(8,128)S(1)}) custom-call(s32[12]{0:T(128)S(1)} %bitcast.22, s32[8,2048]{1,0:T(8,128)S(1)} %bitcast.24, f32[8,2048]{1,0:T(8,128)S(1)} %bitcast.25, bf16[2048,256]{1,0:T(8,128)(2,1)S(1)} %copy-done.1, bf16[1536,256]{1,0:T(8,128)(2,1)S(1)} %bitcast.23), custom_call_target="tpu_custom_call" | custom-call | flops 4294967296 | bytes 23068672 | tf_op jit(solution)/shard_map/build_mixer/pallas_call | solution.py:27
  85.1 1.4 copy-done.2
  86.5 1.4 copy-done.3
  87.8 1.0 copy-done.16
  88.8 20.2 %forward_and_remote_grads.1 = (bf16[2048,256]{1,0:T(8,128)(2,1)}, bf16[2048,256]{1,0:T(8,128)(2,1)}, bf16[64,40,256]{2,1,0:T(8,128)(2,1)}, bf16[1536,256]{1,0:T(8,128)(2,1)}) custom-call(s32[12]{0:T(128)} %bitcast.21, bf16[256,256]{1,0:T(8,128)(2,1)} %weight_ref.3, bf16[2048,256]{1,0:T(8,128)(2,1)} %bitcast.26, bf16[1536,256]{1,0:T(8,128)(2,1)} %all_gather.3.fresh_ref, ...), custom_call_target="tpu_custom_call" | custom-call | tf_op jit(solution)/shard_map/forward_and_remote_grads/pallas_call | solution.py:27
  109.1 15.5 %all-to-all-start.1 = ((bf16[64,40,256]{2,1,0:T(8,128)(2,1)}), bf16[64,40,256]{2,1,0:T(8,128)(2,1)S(1)}, u32[]{:S(2)}, u32[]{:S(2)}) async-start(bf16[64,40,256]{2,1,0:T(8,128)(2,1)} %get-tuple-element.20), calls=%async_computation.1 | async-start | bytes 2621440 | tf_op jit(solution)/shard_map/all_to_all | solution.py:493
  125.4 1.2 copy-done.4
  126.6 5.5 %own_grads.1.local_ref = f32[2048,256]{1,0:T(8,128)S(1)} custom-call(bf16[5632,2048]{1,0:T(8,128)(2,1)} %get-tuple-element.18.mixer_ref, bf16[2048,256]{1,0:T(8,128)(2,1)S(1)} %copy-done.4), custom_call_target="tpu_custom_call" | custom-call | flops 2147483648 | bytes 8388608 | tf_op jit(solution)/shard_map/own_grads/pallas_call | solution.py:27
  132.1 26.7 %all-to-all-done.1 = bf16[64,40,256]{2,1,0:T(8,128)(2,1)S(1)} async-done(((bf16[64,40,256]{2,1,0:T(8,128)(2,1)}), bf16[64,40,256]{2,1,0:T(8,128)(2,1)S(1)}, u32[]{:S(2)}, u32[]{:S(2)}) %all-to-all-start.1) | async-done | bytes 1310752 | tf_op jit(solution)/shard_map/all_to_all | solution.py:493
  158.9 12.7 %all_to_all.20 = f32[12,8,128]{2,1,0:T(8,128)} all-to-all(f32[12,8,128]{2,1,0:T(8,128)S(1)} %broadcast_in_dim.8), channel_id=1, replica_groups=mesh['dom'=64,'grp'=12] {'grp'}, dimensions={0} | all-to-all | bytes 98304 | tf_op jit(solution)/shard_map/all_to_all | solution.py:493
  171.7 1.4 reduce_sum.19
  173.8 0.7 broadcast_in_dim.9
  174.5 7.9 %all-to-all-start.3 = ((f32[64,8,128]{2,1,0:T(8,128)}), f32[64,8,128]{2,1,0:T(8,128)}, u32[]{:S(2)}, u32[]{:S(2)}) async-start(f32[64,8,128]{2,1,0:T(8,128)} %broadcast_in_dim.9), calls=%async_computation.4 | async-start | bytes 524288 | tf_op jit(solution)/shard_map/all_to_all | solution.py:493
  182.4 1.3 fusion.1
  183.7 1.4 copy.16
  185.1 1.4 pad.4.clone
  186.5 0.8 reshape.50.send_ref
  187.4 0.8 copy-done.6
  188.9 6.3 %add_returned_rows.1 = bf16[2048,256]{1,0:T(8,128)(2,1)} custom-call(s32[1,2560]{1,0:T(1,128)S(1)} %reshape.50.send_ref, s32[1,128]{1,0:T(1,128)S(1)} %bitcast.20, f32[2048,256]{1,0:T(8,128)S(1)} %own_grads.1.local_ref, bf16[2560,256]{1,0:T(8,128)(2,1)S(1)} %bitcast.16, bf16[1,128,256]{2,1,0:T(8,128)(2,1)S(1)} %copy-done.6, bf16[256,256]{1,0:T(8,128)(2,1)S(1)} %copy-done.5), custom_call_target="tpu_custom_call" | custom-call | tf_op jit(solution)/shard_map/add_returned_rows/pallas_call | solution.py:27
  195.2 1.7 copy.18
  (38 shorter events, 4.0 us)
Async XLA Ops:
  7.2 1.2 copy-start
  8.4 0.7 copy-start.7
  9.1 0.7 copy-start.9
  9.8 18.3 %copy-start.1 = (bf16[2048,256]{1,0:T(8,128)(2,1)S(1)}, bf16[2048,256]{1,0:T(8,128)(2,1)}, u32[]{:S(2)}) copy-start(bf16[2048,256]{1,0:T(8,128)(2,1)} %feat_ref.5) | copy-start | bytes 3145732
  9.8 18.3 %copy-start.10 = (s32[128]{0:T(128)S(1)}, s32[128]{0:T(128)}, u32[]{:S(2)}) copy-start(s32[128]{0:T(128)} %param.17) | copy-start | bytes 1540
  13.3 45.8 %copy-start.12 = (s32[1,12]{1,0:T(1,128)S(1)}, s32[1,12]{1,0:T(1,128)}, u32[]{:S(2)}) copy-start(s32[1,12]{1,0:T(1,128)} %param.18) | copy-start | bytes 148
  13.3 45.8 %copy-start.13 = (bf16[1,12,128,256]{3,2,1,0:T(8,128)(2,1)S(1)}, bf16[1,12,128,256]{3,2,1,0:T(8,128)(2,1)}, u32[]{:S(2)}) copy-start(bf16[1,12,128,256]{3,2,1,0:T(8,128)(2,1)} %param.19) | copy-start | bytes 2359300
  13.3 45.8 %copy-start.14 = (s32[2048,8]{0,1:T(8,128)S(1)}, s32[2048,8]{0,1:T(8,128)}, u32[]{:S(2)}) copy-start(s32[2048,8]{0,1:T(8,128)} %param.13) | copy-start | bytes 196612
  13.3 45.8 %copy-start.15 = (f32[2048,8]{0,1:T(8,128)S(1)}, f32[2048,8]{0,1:T(8,128)}, u32[]{:S(2)}) copy-start(f32[2048,8]{0,1:T(8,128)} %param.14) | copy-start | bytes 196612
  13.3 74.5 %all-to-all-start = ((bf16[64,32,256]{2,1,0:T(8,128)(2,1)}), bf16[64,32,256]{2,1,0:T(8,128)(2,1)S(1)}, u32[]{:S(2)}, u32[]{:S(2)}) async-start(bf16[64,32,256]{2,1,0:T(8,128)(2,1)} %bitcast.4), calls=%async_computation | async-start | bytes 2097152 | tf_op jit(solution)/shard_map/all_to_all | solution.py:493
  85.1 1.4 copy-start.2
  86.5 1.4 copy-start.3
  87.8 1.0 copy-start.16
  109.1 49.7 %all-to-all-start.1 = ((bf16[64,40,256]{2,1,0:T(8,128)(2,1)}), bf16[64,40,256]{2,1,0:T(8,128)(2,1)S(1)}, u32[]{:S(2)}, u32[]{:S(2)}) async-start(bf16[64,40,256]{2,1,0:T(8,128)(2,1)} %get-tuple-element.20), calls=%async_computation.1 | async-start | bytes 2621440 | tf_op jit(solution)/shard_map/all_to_all | solution.py:493
  124.6 62.7 %reduce-scatter.2.cloned.1.call-start = ((), (), s32[]{:S(2)}) async-start(), calls=%async_computation.5 | async-start | bytes 851968 | tf_op jit(solution)/shard_map/reduce_scatter | solution.py:538
  125.4 1.2 copy-start.4
  132.1 50.3 %copy-start.8 = (s32[64,32]{0,1:T(8,128)S(1)}, s32[64,32]{0,1:T(8,128)}, u32[]{:S(2)}) copy-start(s32[64,32]{0,1:T(8,128)} %param.15) | copy-start | bytes 24580
  132.1 55.2 %copy-start.5 = (bf16[256,256]{1,0:T(8,128)(2,1)S(1)}, bf16[256,256]{1,0:T(8,128)(2,1)}, u32[]{:S(2)}) copy-start(bf16[256,256]{1,0:T(8,128)(2,1)} %weight_ref.3) | copy-start | bytes 393220
  174.5 20.7 %all-to-all-start.3 = ((f32[64,8,128]{2,1,0:T(8,128)}), f32[64,8,128]{2,1,0:T(8,128)}, u32[]{:S(2)}, u32[]{:S(2)}) async-start(f32[64,8,128]{2,1,0:T(8,128)} %broadcast_in_dim.9), calls=%async_computation.4 | async-start | bytes 524288 | tf_op jit(solution)/shard_map/all_to_all | solution.py:493
  187.4 0.8 copy-start.6
  188.2 0.7 copy-start.11
Sparse Core Ops, SparseCore 0:
  128.6 45.3 reduce-scatter.1

commit v4 on v3

--- a/solution.py
+++ b/solution.py
@@ -11,6 +11,7 @@
 BF16 = jnp.bfloat16
 F32 = jnp.float32
 BLOCK = 256
+BUILD_BLOCK = 512
 LANES = 128
 MIB = 1 << 20
 GELU_SCALE = math.sqrt(2.0 / math.pi)
@@ -106,13 +107,13 @@
         sum_ref[...] = jnp.zeros_like(sum_ref)
         stale_ref[...] = jnp.zeros_like(stale_ref)
 
-    row = (lax.broadcasted_iota(jnp.int32, (16, wide), 0) + step * BLOCK).astype(jnp.int16)
+    row = (lax.broadcasted_iota(jnp.int32, (16, wide), 0) + step * BUILD_BLOCK).astype(jnp.int16)
 
     def tile(number, carry):
         lanes = pl.ds(pl.multiple_of(number * wide, wide), wide)
         index = [index_rep[slot, :, lanes] for slot in range(slots)]
         weights = [weight_rep[slot, :, lanes] for slot in range(slots)]
-        for start in range(0, BLOCK, 16):
+        for start in range(0, BUILD_BLOCK, 16):
             here = row + jnp.int16(start)
             value = jnp.zeros((16, wide), BF16)
             for slot in range(slots):
@@ -124,15 +125,15 @@
 
     @pl.when(step < own_blocks)
     def _():
-        rows = pl.ds(pl.multiple_of(step * BLOCK, BLOCK), BLOCK)
+        rows = pl.ds(pl.multiple_of(step * BUILD_BLOCK, BUILD_BLOCK), BUILD_BLOCK)
         sum_ref[...] += contract(mixer_ref[...], feat_ref[rows, :], 0, 0)
 
     @pl.when(step >= panel_blocks)
     def _():
         panel = cached_ref.shape[0] // skip_ref.shape[0]
-        first = (step - panel_blocks) * (BLOCK // panel)
+        first = (step - panel_blocks) * (BUILD_BLOCK // panel)
         pieces = []
-        for part in range(BLOCK // panel):
+        for part in range(BUILD_BLOCK // panel):
             rows = pl.ds(pl.multiple_of((first + part) * panel, panel), panel)
             pieces.append(
                 jnp.where(skip_ref[first + part] == 1, cached_ref[rows, :], jnp.zeros((), BF16))
@@ -361,7 +362,7 @@
     fanout = edge_index.shape[1]
     with jax.named_scope("build_mixer"):
         return call(
-            functools.partial(build_kernel, nodes // BLOCK, (table - cached.shape[0]) // BLOCK),
+            functools.partial(build_kernel, nodes // BUILD_BLOCK, (table - cached.shape[0]) // BUILD_BLOCK),
             (
                 shape((table, nodes), BF16),
                 shape((nodes, width), F32),
@@ -372,7 +373,7 @@
             edge_weight.T,
             features,
             cached,
-            grid=(table // BLOCK,),
+            grid=(table // BUILD_BLOCK,),
             in_specs=[
                 SMEM,
                 whole((fanout, nodes)),
@@ -381,7 +382,7 @@
                 whole(cached.shape),
             ],
             out_specs=[
-                pl.BlockSpec((BLOCK, nodes), lambda step: (step, 0)),
+                pl.BlockSpec((BUILD_BLOCK, nodes), lambda step: (step, 0)),
                 whole((nodes, width)),
                 whole((nodes, width)),
             ],
@@ -540,7 +541,12 @@
     )
     returned = exchange(back, "dom")
     local_grad = own_grads(mixer, grad_pre)
-    returned, local_grad = lax.optimization_barrier((returned, local_grad))
+    extra = back.shape[1] - slots
+    live = lax.broadcasted_iota(jnp.int32, send_rows.shape, 1) < counts[:, None]
+    send_row = jnp.pad(
+        jnp.where(live, send_rows, -1), ((0, 0), (0, extra)), constant_values=-1
+    ).reshape(1, peers * (slots + extra))
+    returned, local_grad, send_row = lax.optimization_barrier((returned, local_grad, send_row))
 
     pairs = returned[:, slots:, :].astype(F32)
     part = jnp.sum(pairs[:, :, :LANES] + pairs[:, :, LANES:], axis=0)
@@ -554,10 +560,6 @@
         .reshape(width, width)
     )
 
-    live = lax.broadcasted_iota(jnp.int32, send_rows.shape, 1) < counts[:, None]
-    send_row = jnp.pad(
-        jnp.where(live, send_rows, -1), ((0, 0), (0, tall)), constant_values=-1
-    ).reshape(1, peers * (slots + tall))
     feature_grad = finish(
         send_row, bound_row, local_grad, returned.reshape(-1, width), owner_grad, weight
     )

time: 205 us -> 200 us (0.976)
  waiting for transfers between devices: 27.4 us -> 31.9 us
  local copies, waits for them, and re-layouts: 15.1 us -> 11 us
  Pallas kernels: 62 us -> 58.7 us
    all_to_all x3, waiting for transfers between devices: 26.7 us -> 31.2 us  [exchange(): return lax.all_to_all(values, axis, split_axis=0, concat_axis=0, tiled=True)]
    pallas_call x6, Pallas kernels: 62 us -> 58.7 us  [call(): return pl.pallas_call(kernel, out_shape=outs, **options)(*operands)]
  transfers between devices with their start and end apart: 4 -> 4, of which waited for: 1 -> 2; matrix products, arithmetic and copies ran while one was open for 4% -> 2% of each run, Pallas kernels for 19% -> 18%
where the time goes in v4:
time: 200 us
  Pallas kernels  58.7 us (29%)
  blocking collectives  43.3 us (22%)
  starting transfers between devices  38.3 us (19%)
  waiting for transfers between devices  31.9 us (16%)
  between operations  14.2 us (7%)
  local copies, waits for them, and re-layouts  11 us (6%)
  other arithmetic  2.21 us (1%)
    pallas_call x6, Pallas kernels, call(): return pl.pallas_call(kernel, out_shape=outs, **options)(*operands)  58.7 us
    all_to_all x3, starting transfers between devices, exchange(): return lax.all_to_all(values, axis, split_axis=0, concat_axis=0, tiled=True)  38.2 us
    all_to_all x3, waiting for transfers between devices, exchange(): return lax.all_to_all(values, axis, split_axis=0, concat_axis=0, tiled=True)  31.2 us
    all_gather x1, blocking collectives, shards(): fresh = lax.all_gather(own_panel, 'grp', axis=0, tiled=True)  30.6 us
    all_to_all x1, blocking collectives, exchange(): return lax.all_to_all(values, axis, split_axis=0, concat_axis=0, tiled=True)  12.7 us
    unnamed x36, local copies, waits for them, and re-layouts  10.1 us
  transfers between devices with their start and end apart: 4, of which 2 were waited for; matrix products, arithmetic and copies ran while one was open for 2% of the time, Pallas kernels for 18%

profile of v4, /device:TPU:1, one launch (start us, length us, event | category | flops | bytes accessed | tf_op | source)
XLA Modules:
  0.0 199.5 jit_solution(5254964604397602506)
XLA Ops:
  7.2 1.2 copy-done
  8.4 0.7 copy-done.7
  9.8 3.5 %gather_sent_rows.1 = bf16[2048,256]{1,0:T(8,128)(2,1)} custom-call(s32[32,64]{1,0:T(8,128)S(1)} %bitcast.17, s32[1,64]{1,0:T(1,128)S(1)} %bitcast.18, bf16[2048,256]{1,0:T(8,128)(2,1)S(1)} %copy-done), custom_call_target="tpu_custom_call" | custom-call | tf_op jit(solution)/shard_map/gather_sent_rows/pallas_call | solution.py:28
  13.3 14.7 %all-to-all-start = ((bf16[64,32,256]{2,1,0:T(8,128)(2,1)}), bf16[64,32,256]{2,1,0:T(8,128)(2,1)S(1)}, u32[]{:S(2)}, u32[]{:S(2)}) async-start(bf16[64,32,256]{2,1,0:T(8,128)(2,1)} %bitcast.4), calls=%async_computation | async-start | bytes 2097152 | tf_op jit(solution)/shard_map/all_to_all | solution.py:494
  28.5 30.6 %all_gather.3.fresh_ref = bf16[1536,256]{1,0:T(8,128)(2,1)} all-gather(bf16[128,256]{1,0:T(8,128)(2,1)S(1)} %gather_panel.1), channel_id=1, replica_groups=mesh['dom'=64,'grp'=12] {'grp'}, dimensions={0}, use_global_device_ids=true | all-gather | bytes 851968 | tf_op jit(solution)/shard_map/all_gather | solution.py:524
  59.1 22.7 %build_mixer.1 = (bf16[5632,2048]{1,0:T(8,128)(2,1)}, f32[2048,256]{1,0:T(8,128)S(1)}, f32[2048,256]{1,0:T(8,128)S(1)}) custom-call(s32[12]{0:T(128)S(1)} %bitcast.22, s32[8,2048]{1,0:T(8,128)S(1)} %bitcast.24, f32[8,2048]{1,0:T(8,128)S(1)} %bitcast.25, bf16[2048,256]{1,0:T(8,128)(2,1)S(1)} %copy-done.1, bf16[1536,256]{1,0:T(8,128)(2,1)S(1)} %bitcast.23), custom_call_target="tpu_custom_call" | custom-call | flops 4294967296 | bytes 23068672 | tf_op jit(solution)/shard_map/build_mixer/pallas_call | solution.py:28
  81.8 1.4 copy-done.2
  83.1 1.4 copy-done.3
  84.5 1.0 copy-done.16
  85.5 20.2 %forward_and_remote_grads.1 = (bf16[2048,256]{1,0:T(8,128)(2,1)}, bf16[2048,256]{1,0:T(8,128)(2,1)}, bf16[64,40,256]{2,1,0:T(8,128)(2,1)}, bf16[1536,256]{1,0:T(8,128)(2,1)}) custom-call(s32[12]{0:T(128)} %bitcast.21, bf16[256,256]{1,0:T(8,128)(2,1)} %weight_ref.3, bf16[2048,256]{1,0:T(8,128)(2,1)} %bitcast.26, bf16[1536,256]{1,0:T(8,128)(2,1)} %all_gather.3.fresh_ref, ...), custom_call_target="tpu_custom_call" | custom-call | tf_op jit(solution)/shard_map/forward_and_remote_grads/pallas_call | solution.py:28
  105.8 15.5 %all-to-all-start.1 = ((bf16[64,40,256]{2,1,0:T(8,128)(2,1)}), bf16[64,40,256]{2,1,0:T(8,128)(2,1)S(1)}, u32[]{:S(2)}, u32[]{:S(2)}) async-start(bf16[64,40,256]{2,1,0:T(8,128)(2,1)} %get-tuple-element.21), calls=%async_computation.1 | async-start | bytes 2621440 | tf_op jit(solution)/shard_map/all_to_all | solution.py:494
  121.4 0.7 reduce-scatter.2.cloned.1.call-update
  122.3 1.2 copy-done.4
  123.5 5.5 %own_grads.1.local_ref = f32[2048,256]{1,0:T(8,128)S(1)} custom-call(bf16[5632,2048]{1,0:T(8,128)(2,1)} %get-tuple-element.19.mixer_ref, bf16[2048,256]{1,0:T(8,128)(2,1)S(1)} %copy-done.4), custom_call_target="tpu_custom_call" | custom-call | flops 2147483648 | bytes 8388608 | tf_op jit(solution)/shard_map/own_grads/pallas_call | solution.py:28
  129.1 26.4 %all-to-all-done.1 = bf16[64,40,256]{2,1,0:T(8,128)(2,1)S(1)} async-done(((bf16[64,40,256]{2,1,0:T(8,128)(2,1)}), bf16[64,40,256]{2,1,0:T(8,128)(2,1)S(1)}, u32[]{:S(2)}, u32[]{:S(2)}) %all-to-all-start.1) | async-done | bytes 1310752 | tf_op jit(solution)/shard_map/all_to_all | solution.py:494
  155.6 12.7 %all_to_all.20 = f32[12,8,128]{2,1,0:T(8,128)} all-to-all(f32[12,8,128]{2,1,0:T(8,128)S(1)} %broadcast_in_dim.9), channel_id=1, replica_groups=mesh['dom'=64,'grp'=12] {'grp'}, dimensions={0} | all-to-all | bytes 98304 | tf_op jit(solution)/shard_map/all_to_all | solution.py:494
  168.4 1.4 reduce_sum.19
  169.8 0.7 broadcast_multiply_fusion
  170.4 0.7 broadcast_in_dim.10
  171.2 7.9 %all-to-all-start.3 = ((f32[64,8,128]{2,1,0:T(8,128)}), f32[64,8,128]{2,1,0:T(8,128)}, u32[]{:S(2)}, u32[]{:S(2)}) async-start(f32[64,8,128]{2,1,0:T(8,128)} %broadcast_in_dim.10), calls=%async_computation.4 | async-start | bytes 524288 | tf_op jit(solution)/shard_map/all_to_all | solution.py:494
  179.2 0.8 copy-done.6
  180.0 6.3 %add_returned_rows.1 = bf16[2048,256]{1,0:T(8,128)(2,1)} custom-call(s32[1,2560]{1,0:T(1,128)S(1)} %reshape.50.send_ref, s32[1,128]{1,0:T(1,128)S(1)} %bitcast.20, f32[2048,256]{1,0:T(8,128)S(1)} %own_grads.1.local_ref, bf16[2560,256]{1,0:T(8,128)(2,1)S(1)} %bitcast.16, bf16[1,128,256]{2,1,0:T(8,128)(2,1)S(1)} %copy-done.6, bf16[256,256]{1,0:T(8,128)(2,1)S(1)} %copy-done.5), custom_call_target="tpu_custom_call" | custom-call | tf_op jit(solution)/shard_map/add_returned_rows/pallas_call | solution.py:28
  186.3 4.7 %all-to-all-done.3 = f32[64,8,128]{2,1,0:T(8,128)} async-done(((f32[64,8,128]{2,1,0:T(8,128)}), f32[64,8,128]{2,1,0:T(8,128)}, u32[]{:S(2)}, u32[]{:S(2)}) %all-to-all-start.3) | async-done | bytes 262176 | tf_op jit(solution)/shard_map/all_to_all | solution.py:494
  191.0 1.7 copy.18
  (38 shorter events, 1.5 us)
Async XLA Ops:
  7.2 1.2 copy-start
  8.4 0.7 copy-start.7
  9.1 0.7 copy-start.9
  9.8 18.3 %copy-start.1 = (bf16[2048,256]{1,0:T(8,128)(2,1)S(1)}, bf16[2048,256]{1,0:T(8,128)(2,1)}, u32[]{:S(2)}) copy-start(bf16[2048,256]{1,0:T(8,128)(2,1)} %feat_ref.5) | copy-start | bytes 3145732
  9.8 18.3 %copy-start.11 = (s32[128]{0:T(128)S(1)}, s32[128]{0:T(128)}, u32[]{:S(2)}) copy-start(s32[128]{0:T(128)} %param.17) | copy-start | bytes 1540
  13.3 45.8 %copy-start.12 = (s32[1,12]{1,0:T(1,128)S(1)}, s32[1,12]{1,0:T(1,128)}, u32[]{:S(2)}) copy-start(s32[1,12]{1,0:T(1,128)} %param.18) | copy-start | bytes 148
  13.3 45.8 %copy-start.13 = (bf16[1,12,128,256]{3,2,1,0:T(8,128)(2,1)S(1)}, bf16[1,12,128,256]{3,2,1,0:T(8,128)(2,1)}, u32[]{:S(2)}) copy-start(bf16[1,12,128,256]{3,2,1,0:T(8,128)(2,1)} %param.19) | copy-start | bytes 2359300
  13.3 45.8 %copy-start.14 = (s32[2048,8]{0,1:T(8,128)S(1)}, s32[2048,8]{0,1:T(8,128)}, u32[]{:S(2)}) copy-start(s32[2048,8]{0,1:T(8,128)} %param.13) | copy-start | bytes 196612
  13.3 45.8 %copy-start.15 = (f32[2048,8]{0,1:T(8,128)S(1)}, f32[2048,8]{0,1:T(8,128)}, u32[]{:S(2)}) copy-start(f32[2048,8]{0,1:T(8,128)} %param.14) | copy-start | bytes 196612
  13.3 71.2 %all-to-all-start = ((bf16[64,32,256]{2,1,0:T(8,128)(2,1)}), bf16[64,32,256]{2,1,0:T(8,128)(2,1)S(1)}, u32[]{:S(2)}, u32[]{:S(2)}) async-start(bf16[64,32,256]{2,1,0:T(8,128)(2,1)} %bitcast.4), calls=%async_computation | async-start | bytes 2097152 | tf_op jit(solution)/shard_map/all_to_all | solution.py:494
  81.8 1.4 copy-start.2
  83.1 1.4 copy-start.3
  84.5 1.0 copy-start.16
  105.8 16.3 %copy-start.8 = (s32[64,32]{0,1:T(8,128)S(1)}, s32[64,32]{0,1:T(8,128)}, u32[]{:S(2)}) copy-start(s32[64,32]{0,1:T(8,128)} %param.15) | copy-start | bytes 24580
  105.8 16.3 %copy-start.10 = (s32[64]{0:T(128)S(1)}, s32[64]{0:T(128)}, u32[]{:S(2)}) copy-start(s32[64]{0:T(128)} %param.16) | copy-start | bytes 772
  105.8 49.7 %all-to-all-start.1 = ((bf16[64,40,256]{2,1,0:T(8,128)(2,1)}), bf16[64,40,256]{2,1,0:T(8,128)(2,1)S(1)}, u32[]{:S(2)}, u32[]{:S(2)}) async-start(bf16[64,40,256]{2,1,0:T(8,128)(2,1)} %get-tuple-element.21), calls=%async_computation.1 | async-start | bytes 2621440 | tf_op jit(solution)/shard_map/all_to_all | solution.py:494
  121.3 57.8 %reduce-scatter.2.cloned.1.call-start = ((), (), s32[]{:S(2)}) async-start(), calls=%async_computation.5 | async-start | bytes 851968 | tf_op jit(solution)/shard_map/reduce_scatter | solution.py:539
  122.3 1.2 copy-start.4
  129.1 50.1 %copy-start.5 = (bf16[256,256]{1,0:T(8,128)(2,1)S(1)}, bf16[256,256]{1,0:T(8,128)(2,1)}, u32[]{:S(2)}) copy-start(bf16[256,256]{1,0:T(8,128)(2,1)} %weight_ref.3) | copy-start | bytes 393220
  171.2 19.9 %all-to-all-start.3 = ((f32[64,8,128]{2,1,0:T(8,128)}), f32[64,8,128]{2,1,0:T(8,128)}, u32[]{:S(2)}, u32[]{:S(2)}) async-start(f32[64,8,128]{2,1,0:T(8,128)} %broadcast_in_dim.10), calls=%async_computation.4 | async-start | bytes 524288 | tf_op jit(solution)/shard_map/all_to_all | solution.py:494
  179.2 0.8 copy-start.6
Sparse Core Ops, SparseCore 0:
  125.3 45.2 reduce-scatter.1
